TPU v7x, 512 devices: a whole 4x4x16 slice. The times are simulated.
512 devices in a mesh: dp: 32 (over y_lo, z), tensor: 16 (over y_hi, x, core).
Axes of the slice: x: 4, y: 4 (y_hi: 2, y_lo: 2; y = y_hi * 2 + y_lo), z: 16, core: 2. Of those that a mesh axis runs over, the one named last changes fastest.
Arguments:
- tokens: bfloat16 [12288, 3072], P(('dp', 'tensor')), may hold values from -6 to 6
- cotangent: bfloat16 [12288, 3072], P(('dp', 'tensor')), may hold values from -0.119628906 to 0.119628906
- up_blocks: bfloat16 [320, 256, 256], P('tensor', 'dp'), may hold values from -0.15625 to 0.15625
- down_blocks: bfloat16 [320, 256, 256], P('tensor', 'dp'), may hold values from -0.078125 to 0.078125
- up_index: int32 [320], P('tensor'), may hold values from 0 to 35, as said below
- up_count: int32 [16], P('tensor'), may hold values from 10 to 20, as said below
- down_index: int32 [320], P('tensor'), may hold values from 0 to 35, as said below
- down_count: int32 [16], P('tensor'), may hold values from 10 to 20, as said below
Outputs:
- mixed: bfloat16 [12288, 3072], P(('dp', 'tensor'))
- up_grad: float32 [320, 256, 256], P('tensor', 'dp')
- down_grad: float32 [320, 256, 256], P('tensor', 'dp')
Inputs may be any that keep to these rules, and one draw needn't show every extreme that they name: `up_index`: the 20 numbers of one tensor shard are distinct. `up_count`: some shard holds exactly 20, another exactly the least. `down_index`: the 20 numbers of one tensor shard are distinct. `down_count`: some shard holds exactly 20, another exactly the least.
All inputs are finite; a program needn't handle non-finite values.
Results may differ from a plain program's by a relative error of at most 0.018.
Values may be sent and summed in bfloat16 or wider, within the bound.
No kernel may reach another device: no remote copies, remote signals or barrier semaphores. Data moves between devices by JAX's collectives and lax.ppermute only.
A program may use at most 64 MiB of HBM per device.

v0:
```python
import jax
import jax.numpy as jnp
from jax import lax
from jax.sharding import PartitionSpec as P

FF = 12288


GELU_C = 0.7978845608028654


def gelu_value(value):
    return 0.5 * value * (1.0 + jnp.tanh(GELU_C * (value + 0.044715 * value * value * value)))


def gelu_slope(value):
    bent = jnp.tanh(GELU_C * (value + 0.044715 * value * value * value))
    return 0.5 * (1.0 + bent) + 0.5 * value * (1.0 - bent * bent) * GELU_C * (
        1.0 + 3.0 * 0.044715 * value * value
    )


def slot_layout(index, count, per_row):
    row_block = index // per_row
    column_block = index % per_row
    live = (jnp.arange(index.shape[0], dtype=jnp.int32) < count).astype(jnp.float32)
    return (row_block, column_block, live)


def one_hot(labels, number, live):
    return (labels[:, None] == jnp.arange(number, dtype=jnp.int32)[None, :]).astype(
        jnp.float32
    ) * live[:, None]


def group_total(received, groups):
    shaped = received.reshape((groups, received.shape[0] // groups) + received.shape[1:])
    return jnp.sum(shaped.astype(jnp.float32), axis=0)


def body(tokens, cotangent, up_blocks, down_blocks, up_index, up_count, down_index, down_count):
    highest = lax.Precision.HIGHEST
    block = up_blocks.shape[2]
    groups = lax.axis_size("dp")
    shards = lax.axis_size("tensor")
    per_row = FF // (block * shards)
    whole = lax.all_gather(tokens, "tensor", axis=0, tiled=True)
    rows, width = whole.shape
    row_blocks = width // block
    up_full, down_full = (
        lax.all_gather(up_blocks, "dp", axis=1, tiled=True),
        lax.all_gather(down_blocks, "dp", axis=1, tiled=True),
    )
    up_row, up_col, up_live = slot_layout(up_index, up_count[0], per_row)
    down_row, down_col, down_live = slot_layout(down_index, down_count[0], per_row)
    x_slots = jnp.take(whole.reshape(rows, row_blocks, block), up_row, axis=1)
    pre_slots = jnp.einsum("tsk,skn->stn", x_slots, up_full, preferred_element_type=jnp.float32)
    pre = jnp.einsum("stn,sh->thn", pre_slots, one_hot(up_col, per_row, up_live), precision=highest)
    hidden = gelu_value(pre).astype(jnp.bfloat16)
    h_slots = jnp.take(hidden, down_col, axis=1)
    down_map = one_hot(down_row, row_blocks, down_live)
    terms = jnp.einsum("tsk,skn->stn", h_slots, down_full, preferred_element_type=jnp.float32)
    placed = jnp.einsum("stn,sd->tdn", terms, down_map, precision=highest)
    mixed = lax.psum_scatter(
        placed.reshape(rows // shards * lax.axis_size("tensor"), width).astype(jnp.bfloat16),
        "tensor",
        scatter_dimension=0,
        tiled=True,
    )
    upstream = lax.all_gather(cotangent, "tensor", axis=0, tiled=True)
    dy_slots = jnp.take(upstream.reshape(rows, row_blocks, block), down_row, axis=1)
    down_terms = jnp.einsum("tsk,tsn->skn", h_slots, dy_slots, preferred_element_type=jnp.float32)
    down_terms = (down_terms * down_live[:, None, None]).astype(jnp.bfloat16)
    back_slots = jnp.einsum("tsn,skn->stk", dy_slots, down_full, preferred_element_type=jnp.float32)
    back = jnp.einsum(
        "stk,sh->thk", back_slots, one_hot(down_col, per_row, down_live), precision=highest
    )
    pre_grad = (back * gelu_slope(pre)).astype(jnp.bfloat16)
    grad_slots = jnp.take(pre_grad, up_col, axis=1)
    up_terms = jnp.einsum("tsk,tsn->skn", x_slots, grad_slots, preferred_element_type=jnp.float32)
    up_terms = (up_terms * up_live[:, None, None]).astype(jnp.bfloat16)
    got_up, got_down = (
        lax.all_to_all(up_terms, "dp", split_axis=1, concat_axis=0, tiled=True),
        lax.all_to_all(down_terms, "dp", split_axis=1, concat_axis=0, tiled=True),
    )
    up_grad = group_total(got_up, groups)
    down_grad = group_total(got_down, groups)
    return (mixed, up_grad, down_grad)


def solution(mesh):
    in_specs = (
        P(("dp", "tensor"), None),
        P(("dp", "tensor"), None),
        P("tensor", "dp", None),
        P("tensor", "dp", None),
        P("tensor"),
        P("tensor"),
        P("tensor"),
        P("tensor"),
    )
    out_specs = (P(("dp", "tensor"), None), P("tensor", "dp", None), P("tensor", "dp", None))
    return jax.shard_map(body, mesh=mesh, in_specs=in_specs, out_specs=out_specs, check_vma=False)
```

profile of v0, /device:TPU:6, one launch (start us, length us, event | category | flops | bytes accessed | tf_op | source)
XLA Modules:
  0.0 709.7 jit_solution(16304053423160760931)
XLA Ops:
  7.2 0.0 all-gather.5.cloned.1.call-start
  7.2 0.7 all-gather.5.cloned.1.call-update
  7.9 0.0 all-gather.11.cloned.1.call-start
  7.9 0.7 all-gather.11.cloned.1.call-update
  8.6 0.0 all-gather.7.cloned.1.call-start
  8.7 0.7 all-gather.7.cloned.1.call-update
  9.4 0.0 all-gather.9.cloned.1.call-start
  9.4 0.5 all-gather.9.cloned.1.call-update
  11.3 0.7 compare_and_fusion.1
  12.0 0.7 compare_and_fusion
  12.7 67.6 %all-gather.5.cloned.1.call-done = bf16[384,3072]{1,0:T(8,128)(2,1)} async-done(((bf16[24,3072]{1,0:T(8,128)(2,1)}), bf16[384,3072]{1,0:T(8,128)(2,1)}) %all-gather.5.cloned.1.call-update) | async-done | bytes 2359312 | tf_op jit(solution)/shard_map/all_gather | solution.py:47
  80.3 4.3 copy.55
  84.5 2.8 copy.56
  87.3 59.9 %all-gather.11.cloned.1.call-done = bf16[384,3072]{1,0:T(8,128)(2,1)} async-done(((bf16[24,3072]{1,0:T(8,128)(2,1)}), bf16[384,3072]{1,0:T(8,128)(2,1)}) %all-gather.11.cloned.1.call-update) | async-done | bytes 2359312 | tf_op jit(solution)/shard_map/all_gather | solution.py:70
  147.3 4.3 copy.61
  151.6 4.3 copy.62
  155.8 2.9 gather_fusion
  158.7 4.5 gather_fusion.2
  163.3 116.7 %all-gather.7.cloned.1.call-done = bf16[20,256,256]{2,1,0:T(8,128)(2,1)} async-done(((bf16[20,8,256]{2,1,0:T(8,128)(2,1)}), bf16[20,256,256]{2,1,0:T(8,128)(2,1)}) %all-gather.7.cloned.1.call-update) | async-done | bytes 2621456 | tf_op jit(solution)/shard_map/all_gather | solution.py:51
  280.0 4.2 fusion.16
  284.2 9.9 %fusion.4 = f32[3,384,256]{2,0,1:T(4,128)S(1)} fusion(f32[20,384,256]{2,1,0:T(8,128)S(1)} %fusion.16, f32[20]{0:T(128)S(1)} %compare_convert_fusion, s32[20]{0:T(128)S(1)} %get-tuple-element.18), kind=kOutput, calls=%fused_computation.8 | convolution fusion | flops 70779000 | bytes 9044128 | tf_op jit(solution)/shard_map/stn,sh->thn/dot_general | solution.py:58
  294.1 115.5 %all-gather.9.cloned.1.call-done = bf16[20,256,256]{2,1,0:T(8,128)(2,1)} async-done(((bf16[20,8,256]{2,1,0:T(8,128)(2,1)}), bf16[20,256,256]{2,1,0:T(8,128)(2,1)}) %all-gather.9.cloned.1.call-update) | async-done | bytes 2621456 | tf_op jit(solution)/shard_map/all_gather | solution.py:52
  409.7 4.2 fusion.10
  413.9 9.6 %fusion = f32[3,384,256]{2,0,1:T(4,128)S(1)} fusion(f32[20,384,256]{2,1,0:T(8,128)S(1)} %fusion.10, f32[20]{0:T(128)S(1)} %compare_convert_fusion.1, s32[20]{0:T(128)S(1)} %get-tuple-element.28), kind=kOutput, calls=%fused_computation.4 | convolution fusion | flops 70779000 | bytes 9044128 | tf_op jit(solution)/shard_map/stk,sh->thk/dot_general | solution.py:75
  423.5 1.2 fusion.37
  424.6 3.0 gather_fusion.3
  427.6 5.2 multiply_convert_fusion.1
  432.8 3.3 copy.66
  436.1 8.1 %all-to-all-start = ((bf16[20,256,256]{2,0,1:T(8,128)(2,1)}), bf16[20,256,256]{2,0,1:T(8,128)(2,1)}, u32[]{:S(2)}, u32[]{:S(2)}) async-start(bf16[20,256,256]{2,0,1:T(8,128)(2,1)} %copy.66), calls=%async_computation | async-start | bytes 6291456 | tf_op jit(solution)/shard_map/all_to_all | solution.py:83
  444.2 2.9 gather_fusion.1
  447.2 5.2 multiply_convert_fusion
  452.4 3.2 copy.68
  455.5 109.2 %all-to-all-done = bf16[20,256,256]{2,0,1:T(8,128)(2,1)} async-done(((bf16[20,256,256]{2,0,1:T(8,128)(2,1)}), bf16[20,256,256]{2,0,1:T(8,128)(2,1)}, u32[]{:S(2)}, u32[]{:S(2)}) %all-to-all-start) | async-done | bytes 2621472 | tf_op jit(solution)/shard_map/all_to_all | solution.py:83
  564.7 14.2 %all-to-all-start.1 = ((bf16[20,256,256]{2,0,1:T(8,128)(2,1)}), bf16[20,256,256]{2,0,1:T(8,128)(2,1)S(1)}, u32[]{:S(2)}, u32[]{:S(2)}) async-start(bf16[20,256,256]{2,0,1:T(8,128)(2,1)} %copy.68), calls=%async_computation.1 | async-start | bytes 6291456 | tf_op jit(solution)/shard_map/all_to_all | solution.py:84
  578.9 0.0 reduce-scatter.4.cloned.1.call-start
  579.0 4.2 fusion.13
  583.2 11.3 %convert_bitcast_fusion = bf16[384,12,256]{2,1,0:T(8,128)(2,1)} fusion(f32[20,384,256]{2,1,0:T(8,128)S(1)} %fusion.13, f32[20]{0:T(128)S(1)} %compare_convert_fusion.1, s32[20]{0:T(128)S(1)} %get-tuple-element.20), kind=kOutput, calls=%fused_computation.31 | convolution fusion | flops 284295648 | bytes 10223776 | tf_op jit(solution)/shard_map/stn,sd->tdn/dot_general | solution.py:63
  594.5 4.8 copy.60
  599.4 4.3 copy.74
  603.7 0.0 reduce-scatter.4.cloned.1.call-update
  603.7 2.4 convert_reduce_fusion.1
  606.1 0.7 copy.70
  606.8 91.2 %all-to-all-done.1 = bf16[20,256,256]{2,0,1:T(8,128)(2,1)S(1)} async-done(((bf16[20,256,256]{2,0,1:T(8,128)(2,1)}), bf16[20,256,256]{2,0,1:T(8,128)(2,1)S(1)}, u32[]{:S(2)}, u32[]{:S(2)}) %all-to-all-start.1) | async-done | bytes 2621472 | tf_op jit(solution)/shard_map/all_to_all | solution.py:84
  698.0 0.5 convert_reduce_fusion
  698.5 0.7 copy.71
  699.2 3.7 reduce-scatter.4.cloned.1.call-done
  (9 shorter events, 0.0 us)
Async XLA Ops:
  7.2 73.1 %all-gather.5.cloned.1.call-start = ((), (), s32[]{:S(2)}) async-start(), calls=%async_computation.3 | async-start | bytes 2506752 | tf_op jit(solution)/shard_map/all_gather | solution.py:47
  7.9 139.4 %all-gather.11.cloned.1.call-start = ((), (), s32[]{:S(2)}) async-start(), calls=%async_computation.6 | async-start | bytes 2506752 | tf_op jit(solution)/shard_map/all_gather | solution.py:70
  8.6 271.4 %all-gather.7.cloned.1.call-start = ((), (), s32[]{:S(2)}) async-start(), calls=%async_computation.4 | async-start | bytes 2703360 | tf_op jit(solution)/shard_map/all_gather | solution.py:51
  9.4 400.3 %all-gather.9.cloned.1.call-start = ((), (), s32[]{:S(2)}) async-start(), calls=%async_computation.5 | async-start | bytes 2703360 | tf_op jit(solution)/shard_map/all_gather | solution.py:52
  436.1 128.6 %all-to-all-start = ((bf16[20,256,256]{2,0,1:T(8,128)(2,1)}), bf16[20,256,256]{2,0,1:T(8,128)(2,1)}, u32[]{:S(2)}, u32[]{:S(2)}) async-start(bf16[20,256,256]{2,0,1:T(8,128)(2,1)} %copy.66), calls=%async_computation | async-start | bytes 6291456 | tf_op jit(solution)/shard_map/all_to_all | solution.py:83
  564.7 133.3 %all-to-all-start.1 = ((bf16[20,256,256]{2,0,1:T(8,128)(2,1)}), bf16[20,256,256]{2,0,1:T(8,128)(2,1)S(1)}, u32[]{:S(2)}, u32[]{:S(2)}) async-start(bf16[20,256,256]{2,0,1:T(8,128)(2,1)} %copy.68), calls=%async_computation.1 | async-start | bytes 6291456 | tf_op jit(solution)/shard_map/all_to_all | solution.py:84
  578.9 124.0 %reduce-scatter.4.cloned.1.call-start = ((), (), s32[]{:S(2)}) async-start(), calls=%async_computation.7 | async-start | bytes 2506752
Sparse Core Ops, SparseCore 0:
  11.3 68.9 all-gather.4
  83.6 63.6 all-gather.10
  149.3 130.6 all-gather.6
  281.9 127.7 all-gather.8
  603.8 99.1 reduce-scatter.3
where the time goes:
time: 721 us; the launch traced here: 710 us
  waiting for transfers between devices  567 us (79%)
  matrix products  53.8 us (7%)
  local copies, waits for them, and re-layouts  46 us (6%)
  starting transfers between devices  22.6 us (3%)
  between operations  15.4 us (2%)
    all_gather x1, waiting for transfers between devices, body(): lax.all_gather(up_blocks, 'dp', axis=1, tiled=True)  117 us
    all_gather x1, waiting for transfers between devices, body(): lax.all_gather(down_blocks, 'dp', axis=1, tiled=True)  116 us
    all_to_all x1, waiting for transfers between devices, body(): lax.all_to_all(up_terms, 'dp', split_axis=1, concat_axis=0, tiled=True)  109 us
    all_to_all x1, waiting for transfers between devices, body(): lax.all_to_all(down_terms, 'dp', split_axis=1, concat_axis=0, tiled=True)  91.2 us
    all_gather x1, waiting for transfers between devices, body(): whole = lax.all_gather(tokens, 'tensor', axis=0, tiled=True)  67.6 us
    all_gather x1, waiting for transfers between devices, body(): upstream = lax.all_gather(cotangent, 'tensor', axis=0, tiled=True)  59.9 us
  transfers between devices with their start and end apart: 7, of which 7 were waited for; matrix products, arithmetic and copies ran while one was open for 11% of the time, Pallas kernels for 0%

commit v1 on v0

v1 whole, which is shorter than its diff:
```python
import functools

import jax
import jax.numpy as jnp
from jax import lax
from jax.experimental import pallas as pl
from jax.experimental.pallas import tpu as pltpu
from jax.sharding import PartitionSpec as P

FF = 12288
GELU_C = 0.7978845608028654
VMEM_BYTES = 52 * 1024 * 1024


def bent_tanh(value):
    return jnp.tanh(GELU_C * (value + 0.044715 * value * value * value))


def gelu_slope(value, bent):
    return 0.5 * (1.0 + bent) + 0.5 * value * (1.0 - bent * bent) * GELU_C * (
        1.0 + 3.0 * 0.044715 * value * value
    )


def slot_rows(slices):
    ring, both, columns = slices.shape
    wide = slices.astype(jnp.float32)
    half = both // 2
    first = wide[:, :half].reshape(ring * half, columns)
    second = wide[:, half:].reshape(ring * half, columns)
    return jnp.concatenate([first, second], axis=0).astype(jnp.bfloat16)


def ring_rows(block, ring, both):
    half = both // 2
    rows, columns = block.shape
    first = block[: rows // 2].reshape(ring, half, columns)
    second = block[rows // 2 :].reshape(ring, half, columns)
    return jnp.concatenate([first, second], axis=1).astype(jnp.bfloat16)


def span(number, block):
    return pl.ds(pl.multiple_of(number * block, block), block)


def place_up(index, count, slots, dense, per_row):
    block = slots.shape[-1]
    dense[...] = jnp.zeros_like(dense)

    def place(s, _):
        row, column = lax.div(index[s], per_row), lax.rem(index[s], per_row)
        dense[span(row, block), span(column, block)] = slot_rows(slots[:, s])
        return 0

    lax.fori_loop(0, count[0], place, 0)


def place_down(index, count, slots, first, dense, per_row):
    block = slots.shape[-1]
    dense[...] = jnp.zeros_like(dense)

    def place(s, _):
        row, column = lax.div(index[s], per_row), lax.rem(index[s], per_row)
        dense[span(column, block), span(row, block)] = slot_rows(slots[:, first + s])
        return 0

    lax.fori_loop(0, count[0], place, 0)


def terms_kernel(
    up_index, up_count, down_index, down_count, x, x_t, dy, slots, terms, hidden, up, down, grad, hidden_t
):
    ring, both_slots, both, block = slots.shape
    cap = both_slots // 2
    per_row = up.shape[1] // block
    place_up(up_index, up_count, slots, up, per_row)
    place_down(down_index, down_count, slots, cap, down, per_row)
    for column in range(per_row):
        part = slice(column * block, (column + 1) * block)
        pre = jnp.dot(x[...], up[:, part], preferred_element_type=jnp.float32)
        bent = bent_tanh(pre)
        unit = 0.5 * pre * (1.0 + bent)
        hidden[:, part] = unit.astype(jnp.bfloat16)
        hidden_t[part, :] = jnp.transpose(unit).astype(jnp.bfloat16)
        back = lax.dot_general(
            dy[...], down[part, :], (((1,), (1,)), ((), ())), preferred_element_type=jnp.float32
        )
        grad[column] = (back * gelu_slope(pre, bent)).astype(jnp.bfloat16)

    def term(s, _):
        row, column = lax.div(down_index[s], per_row), lax.rem(down_index[s], per_row)
        live = (s < down_count[0]).astype(jnp.float32)
        value = jnp.dot(
            hidden_t[span(column, block), :], dy[:, span(row, block)], preferred_element_type=jnp.float32
        )
        terms[:, cap + s] = ring_rows(value * live, ring, both)
        row, column = lax.div(up_index[s], per_row), lax.rem(up_index[s], per_row)
        live = (s < up_count[0]).astype(jnp.float32)
        value = jnp.dot(x_t[span(row, block), :], grad[column], preferred_element_type=jnp.float32)
        terms[:, s] = ring_rows(value * live, ring, both)
        return 0

    lax.fori_loop(0, cap, term, 0, unroll=2)


def partial_kernel(down_index, down_count, hidden, slots, out, down):
    cap, block = slots.shape[1] // 2, slots.shape[3]
    per_row = hidden.shape[1] // block
    place_down(down_index, down_count, slots, cap, down, per_row)
    step = 2 * block
    for at in range(0, out.shape[1], step):
        out[:, at : at + step] = jnp.dot(
            hidden[...], down[:, at : at + step], preferred_element_type=jnp.float32
        ).astype(jnp.bfloat16)


SCALARS = pl.BlockSpec(memory_space=pltpu.SMEM)
WHOLE = pl.BlockSpec(memory_space=pltpu.VMEM)


def all_terms(up_index, up_count, down_index, down_count, x, x_t, dy, slots, units):
    rows, width = x.shape
    block = slots.shape[3]
    flops = 2 * rows * width * units * 2 + 2 * rows * block * block * slots.shape[1]
    return pl.pallas_call(
        terms_kernel,
        out_shape=(
            jax.ShapeDtypeStruct(slots.shape, jnp.bfloat16),
            jax.ShapeDtypeStruct((rows, units), jnp.bfloat16),
        ),
        in_specs=[SCALARS] * 4 + [WHOLE] * 4,
        out_specs=(WHOLE, WHOLE),
        scratch_shapes=[
            pltpu.VMEM((width, units), jnp.bfloat16),
            pltpu.VMEM((units, width), jnp.bfloat16),
            pltpu.VMEM((units // block, rows, block), jnp.bfloat16),
            pltpu.VMEM((units, rows), jnp.bfloat16),
        ],
        compiler_params=pltpu.CompilerParams(vmem_limit_bytes=VMEM_BYTES),
        cost_estimate=pl.CostEstimate(flops=flops, bytes_accessed=4 * slots.size, transcendentals=rows * units),
        name="terms",
    )(up_index, up_count, down_index, down_count, x, x_t, dy, slots)


def partial_sum(down_index, down_count, hidden, slots, width):
    rows, units = hidden.shape
    return pl.pallas_call(
        partial_kernel,
        out_shape=jax.ShapeDtypeStruct((rows, width), jnp.bfloat16),
        in_specs=[SCALARS] * 2 + [WHOLE] * 2,
        out_specs=WHOLE,
        scratch_shapes=[pltpu.VMEM((units, width), jnp.bfloat16)],
        compiler_params=pltpu.CompilerParams(vmem_limit_bytes=VMEM_BYTES),
        cost_estimate=pl.CostEstimate(
            flops=2 * rows * units * width, bytes_accessed=2 * slots.size, transcendentals=0
        ),
        name="partial",
    )(down_index, down_count, hidden, slots)


def spread(value, shards):
    copies = jnp.broadcast_to(value[None], (shards,) + value.shape)
    got = lax.all_to_all(copies, "tensor", split_axis=0, concat_axis=0, tiled=True)
    return got.reshape((shards * value.shape[0],) + value.shape[1:])


def body(tokens, cotangent, up_blocks, down_blocks, up_index, up_count, down_index, down_count):
    cap, part, block = up_blocks.shape
    groups = lax.axis_size("dp")
    shards = lax.axis_size("tensor")
    ring = groups // 2
    rings = [list(range(ring)), list(range(ring, groups))]
    across = [(i, (i + ring) % groups) for i in range(groups)]
    upper = lax.axis_index("dp") >= ring
    own = jnp.concatenate([up_blocks, down_blocks], axis=0)
    other = lax.ppermute(own, "dp", across)
    pair = jnp.concatenate(
        [jnp.where(upper, other, own), jnp.where(upper, own, other)], axis=1
    )
    slots = lax.all_gather(
        pair.reshape(2 * cap * 2 * part, block), "dp", axis=0, tiled=True, axis_index_groups=rings
    ).reshape(ring, 2 * cap, 2 * part, block)
    x = spread(tokens, shards)
    dy = spread(cotangent, shards)
    rows, width = x.shape
    terms, hidden = all_terms(
        up_index, up_count, down_index, down_count, x, x.T, dy, slots, FF // shards
    )
    summed = lax.psum_scatter(
        terms.reshape(ring * 2 * cap * 2 * part, block),
        "dp",
        scatter_dimension=0,
        tiled=True,
        axis_index_groups=rings,
    ).reshape(2 * cap, 2 * part, block)
    value = partial_sum(down_index, down_count, hidden, slots, width)
    got = lax.all_to_all(
        value.reshape(shards, rows // shards, width), "tensor", split_axis=0, concat_axis=0, tiled=True
    )
    mixed = jnp.sum(got.astype(jnp.float32), axis=0).astype(jnp.bfloat16)
    low, high = summed[:, :part], summed[:, part:]
    far = lax.ppermute(jnp.where(upper, low, high), "dp", across)
    grads = jnp.where(upper, high, low).astype(jnp.float32) + far.astype(jnp.float32)
    return (mixed, grads[:cap], grads[cap:])


def solution(mesh):
    in_specs = (
        P(("dp", "tensor"), None),
        P(("dp", "tensor"), None),
        P("tensor", "dp", None),
        P("tensor", "dp", None),
        P("tensor"),
        P("tensor"),
        P("tensor"),
        P("tensor"),
    )
    out_specs = (P(("dp", "tensor"), None), P("tensor", "dp", None), P("tensor", "dp", None))
    return jax.shard_map(body, mesh=mesh, in_specs=in_specs, out_specs=out_specs, check_vma=False)
```

time: 721 us -> 216 us (0.30); the launches traced: 710 us -> 216 us
  waiting for transfers between devices: 567 us -> 107 us
  matrix products: 53.8 us -> 0 us
  local copies, waits for them, and re-layouts: 46 us -> 8.18 us
  blocking collectives: 0 us -> 37.4 us
  Pallas kernels: 0 us -> 24.1 us
    all_gather x4 -> x1, waiting for transfers between devices: 360 us -> 8.9 us  [body(): lax.all_gather(pair.reshape(2 * cap * 2 * part, block), 'dp', axis=0, til...]
    all_to_all x2, waiting for transfers between devices: 200 us -> 25.6 us  [the longest x1 25.6 us: spread(): lax.all_to_all(copies, 'tensor', split_axis=0, concat_axis=0, tiled=True)]
    reduce_scatter x0 -> x1, waiting for transfers between devices: none -> 65.1 us  [body(): lax.psum_scatter(terms.reshape(ring * 2 * cap * 2 * part, block), 'dp', s...]
    dot_general x8 -> x0, matrix products: 53.8 us -> none  [the longest x1 11.3 us: body(): placed = jnp.einsum('stn,sd->tdn', terms, down_map, precision=highest)]
    all_to_all x0 -> x1, blocking collectives: none -> 37.4 us  [spread(): lax.all_to_all(copies, 'tensor', split_axis=0, concat_axis=0, tiled=True)]
    pallas_call x0 -> x2, Pallas kernels: none -> 24.1 us  [the longest x1 17.4 us: all_terms(): pl.pallas_call(terms_kernel, out_shape=(jax.ShapeDtypeStruct(slots.shape,...]
    gather x4 -> x0, local copies, waits for them, and re-layouts: 13.3 us -> none  [the longest x1 4.55 us: body(): jnp.take(upstream.reshape(rows, row_blocks, block), down_row, axis=1)]
    convert_element_type x3 -> x0, local copies, waits for them, and re-layouts: 11.3 us -> none  [the longest x1 4.83 us: body(): placed.reshape(rows // shards * lax.axis_size('tensor'), width)]
  transfers between devices with their start and end apart: 7 -> 6, of which waited for: 7 -> 5; matrix products, arithmetic and copies ran while one was open for 11% -> 4% of each run, Pallas kernels for 0% -> 3%
where the time goes in v1:
time: 216 us
  waiting for transfers between devices  107 us (50%)
  blocking collectives  37.4 us (17%)
  Pallas kernels  24.1 us (11%)
  starting transfers between devices  20.9 us (10%)
  between operations  15.4 us (7%)
  local copies, waits for them, and re-layouts  8.18 us (4%)
  other arithmetic  2.96 us (1%)
    reduce_scatter x1, waiting for transfers between devices, body(): lax.psum_scatter(terms.reshape(ring * 2 * cap * 2 * part, block), 'dp', s...  65.1 us
    all_to_all x1, blocking collectives, spread(): lax.all_to_all(copies, 'tensor', split_axis=0, concat_axis=0, tiled=True)  37.4 us
    all_to_all x1, waiting for transfers between devices, spread(): lax.all_to_all(copies, 'tensor', split_axis=0, concat_axis=0, tiled=True)  25.6 us
    pallas_call x1, Pallas kernels, all_terms(): pl.pallas_call(terms_kernel, out_shape=(jax.ShapeDtypeStruct(slots.shape,...  17.4 us
    all_gather x1, waiting for transfers between devices, body(): lax.all_gather(pair.reshape(2 * cap * 2 * part, block), 'dp', axis=0, til...  8.9 us
    all_to_all x1, starting transfers between devices, body(): lax.all_to_all(value.reshape(shards, rows // shards, width), 'tensor', sp...  7.37 us
    pallas_call x1, Pallas kernels, partial_sum(): pl.pallas_call(partial_kernel, out_shape=jax.ShapeDtypeStruct((rows, widt...  6.72 us
    all_to_all x1, starting transfers between devices, spread(): lax.all_to_all(copies, 'tensor', split_axis=0, concat_axis=0, tiled=True)  6.67 us
  transfers between devices with their start and end apart: 6, of which 5 were waited for; matrix products, arithmetic and copies ran while one was open for 4% of the time, Pallas kernels for 3%

profile of v1, /device:TPU:6, one launch (start us, length us, event | category | flops | bytes accessed | tf_op | source)
XLA Modules:
  0.0 215.8 jit_solution(13732636636442261007)
XLA Ops:
  7.2 0.0 all-gather.2.cloned.1.call-start
  7.2 0.9 constant_dynamic-update-slice_fusion.1
  8.1 0.9 constant_dynamic-update-slice_fusion
  9.0 3.5 %collective-permute-start = (bf16[40,8,256]{2,1,0:T(8,128)(2,1)S(1)}, bf16[40,8,256]{2,1,0:T(8,128)(2,1)S(1)}, u32[]{:S(2)}, u32[]{:S(2)}) collective-permute-start(bf16[40,8,256]{2,1,0:T(8,128)(2,1)S(1)} %constant_dynamic-update-slice_fusion), channel_id=1, source_target_pairs={{0,256},{16,272},{32,288},{48,304},{64,320},{80,336},{96,352},{112... | collective-permute-start | bytes 491528 | tf_op jit(solution)/shard_map/ppermute | solution.py:176
  12.5 4.3 %collective-permute-done = bf16[40,8,256]{2,1,0:T(8,128)(2,1)S(1)} collective-permute-done((bf16[40,8,256]{2,1,0:T(8,128)(2,1)S(1)}, bf16[40,8,256]{2,1,0:T(8,128)(2,1)S(1)}, u32[]{:S(2)}, u32[]{:S(2)}) %collective-permute-start) | collective-permute-done | bytes 163872 | tf_op jit(solution)/shard_map/ppermute | solution.py:176
  16.8 0.8 pad_maximum_fusion
  17.6 0.0 all-gather.2.cloned.1.call-update
  17.6 1.2 broadcast_in_dim.4
  18.8 0.0 copy-start.4
  18.8 37.4 %all_to_all.15 = bf16[16,24,3072]{2,1,0:T(8,128)(2,1)S(1)} all-to-all(bf16[16,24,3072]{2,1,0:T(8,128)(2,1)S(1)} %broadcast_in_dim.4), channel_id=1, replica_groups=mesh['dp'=32,'tensor'=16] {'tensor'}, dimensions={0} | all-to-all | bytes 4718592 | tf_op jit(solution)/shard_map/all_to_all | solution.py:163
  56.2 0.0 copy-done.4
  56.2 0.0 copy-start.2
  56.2 2.0 broadcast_in_dim.5
  58.2 6.7 %all-to-all-start.1 = ((bf16[16,24,3072]{2,1,0:T(8,128)(2,1)}), bf16[16,24,3072]{2,1,0:T(8,128)(2,1)}, u32[]{:S(2)}, u32[]{:S(2)}) async-start(bf16[16,24,3072]{2,1,0:T(8,128)(2,1)} %broadcast_in_dim.5), calls=%async_computation.1 | async-start | bytes 4718592 | tf_op jit(solution)/shard_map/all_to_all | solution.py:163
  64.8 0.0 reduce-scatter.2.cloned.1.call-start
  66.2 0.0 copy-done.2
  66.2 0.0 copy-start
  66.2 0.0 copy-start.1
  66.2 2.5 %copy.13 = bf16[384,3072]{0,1:T(8,128)(2,1)} copy(bf16[384,3072]{1,0:T(8,128)(2,1)S(1)} %bitcast.8) | data formatting | bytes 4718592 | tf_op jit(solution)/shard_map/reshape | solution.py:164
  68.7 25.6 %all-to-all-done.1 = bf16[16,24,3072]{2,1,0:T(8,128)(2,1)} async-done(((bf16[16,24,3072]{2,1,0:T(8,128)(2,1)}), bf16[16,24,3072]{2,1,0:T(8,128)(2,1)}, u32[]{:S(2)}, u32[]{:S(2)}) %all-to-all-start.1) | async-done | bytes 2359328 | tf_op jit(solution)/shard_map/all_to_all | solution.py:163
  94.3 8.9 %all-gather.2.cloned.1.call-done = bf16[10240,256]{1,0:T(8,128)(2,1)} async-done(((bf16[640,256]{1,0:T(8,128)(2,1)}), bf16[10240,256]{1,0:T(8,128)(2,1)}) %all-gather.2.cloned.1.call-update) | async-done | bytes 5242896 | tf_op jit(solution)/shard_map/all_gather | solution.py:180
  103.2 0.0 copy-done
  103.2 0.0 copy-done.1
  103.2 17.4 %terms.1 = (bf16[16,40,16,256]{3,2,1,0:T(8,128)(2,1)}, bf16[384,768]{1,0:T(8,128)(2,1)S(1)}) custom-call(s32[20]{0:T(128)S(1)} %copy-done.1, s32[1]{0:T(128)S(6)} %copy.15.up_count, s32[20]{0:T(128)S(1)} %copy-done, s32[1]{0:T(128)S(6)} %copy.16.down_count, bf16[384,3072]{1,0:T(8,128)(2,1)} %bitcast.9, bf16[3072,384]{1,0:T(8,128)(2,1)} %bitcast.14, ...), custom_call_target="tpu_custom_call" | custom-call | flops 5637144576 | bytes 10485760 | tf_op jit(solution)/shard_map/terms/pallas_call | solution.py:125
  120.7 0.0 reduce-scatter.2.cloned.1.call-update
  120.7 6.7 %partial.1 = bf16[384,3072]{1,0:T(8,128)(2,1)} custom-call(s32[20]{0:T(128)S(1)} %copy-done, s32[1]{0:T(128)S(6)} %copy.16.down_count, bf16[384,768]{1,0:T(8,128)(2,1)S(1)} %get-tuple-element.5.hidden, bf16[16,40,16,256]{3,2,1,0:T(8,128)(2,1)} %bitcast.12), custom_call_target="tpu_custom_call" | custom-call | flops 1811939328 | bytes 5242880 | tf_op jit(solution)/shard_map/partial/pallas_call | solution.py:147
  127.4 7.4 %all-to-all-start.2 = ((bf16[16,24,3072]{2,1,0:T(8,128)(2,1)}), bf16[16,24,3072]{2,1,0:T(8,128)(2,1)S(1)}, u32[]{:S(2)}, u32[]{:S(2)}) async-start(bf16[16,24,3072]{2,1,0:T(8,128)(2,1)} %bitcast.10), calls=%async_computation.2 | async-start | bytes 4718592 | tf_op jit(solution)/shard_map/all_to_all | solution.py:197
  134.8 65.1 %reduce-scatter.2.cloned.1.call-done = bf16[640,256]{1,0:T(8,128)(2,1)} async-done(((bf16[10240,256]{1,0:T(8,128)(2,1)}), bf16[640,256]{1,0:T(8,128)(2,1)}) %reduce-scatter.2.cloned.1.call-update) | async-done | bytes 327696 | tf_op jit(solution)/shard_map/reduce_scatter | solution.py:189
  199.9 0.0 copy-start.3
  199.9 1.1 broadcast_select_fusion
  201.0 3.3 %collective-permute-start.1 = (bf16[40,8,256]{2,1,0:T(8,128)(2,1)S(1)}, bf16[40,8,256]{2,1,0:T(8,128)(2,1)S(1)}, u32[]{:S(2)}, u32[]{:S(2)}) collective-permute-start(bf16[40,8,256]{2,1,0:T(8,128)(2,1)S(1)} %broadcast_select_fusion), channel_id=1, source_target_pairs={{0,256},{16,272},{32,288},{48,304},{64,320},{80,336},{96,352},{112... | collective-permute-start | bytes 491528 | tf_op jit(solution)/shard_map/ppermute | solution.py:202
  204.3 0.0 all-to-all-done.2
  204.3 1.1 reduce_sum.12
  205.4 2.8 %collective-permute-done.1 = bf16[40,8,256]{2,1,0:T(8,128)(2,1)S(1)} collective-permute-done((bf16[40,8,256]{2,1,0:T(8,128)(2,1)S(1)}, bf16[40,8,256]{2,1,0:T(8,128)(2,1)S(1)}, u32[]{:S(2)}, u32[]{:S(2)}) %collective-permute-start.1) | collective-permute-done | bytes 163872 | tf_op jit(solution)/shard_map/ppermute | solution.py:202
  208.2 0.0 copy-done.3
  208.2 0.1 convert_add_fusion
  208.2 0.7 fusion
  (1 shorter events, 0.0 us)
Async XLA Ops:
  7.2 96.1 %all-gather.2.cloned.1.call-start = ((), (), s32[]{:S(2)}) async-start(), calls=%async_computation.4 | async-start | bytes 5570560 | tf_op jit(solution)/shard_map/all_gather | solution.py:180
  9.0 7.8 %collective-permute-start = (bf16[40,8,256]{2,1,0:T(8,128)(2,1)S(1)}, bf16[40,8,256]{2,1,0:T(8,128)(2,1)S(1)}, u32[]{:S(2)}, u32[]{:S(2)}) collective-permute-start(bf16[40,8,256]{2,1,0:T(8,128)(2,1)S(1)} %constant_dynamic-update-slice_fusion), channel_id=1, source_target_pairs={{0,256},{16,272},{32,288},{48,304},{64,320},{80,336},{96,352},{112... | collective-permute-start | bytes 491528 | tf_op jit(solution)/shard_map/ppermute | solution.py:176
  18.8 37.4 %copy-start.4 = (bf16[24,3072]{1,0:T(8,128)(2,1)S(1)}, bf16[24,3072]{1,0:T(8,128)(2,1)}, u32[]{:S(2)}) copy-start(bf16[24,3072]{1,0:T(8,128)(2,1)} %param.9) | copy-start | bytes 442372
  56.2 10.0 %copy-start.2 = (bf16[16,24,3072]{2,1,0:T(8,128)(2,1)}, bf16[16,24,3072]{2,1,0:T(8,128)(2,1)S(1)}, u32[]{:S(2)}) copy-start(bf16[16,24,3072]{2,1,0:T(8,128)(2,1)S(1)} %all_to_all.15) | copy-start | bytes 7077892
  58.2 36.2 %all-to-all-start.1 = ((bf16[16,24,3072]{2,1,0:T(8,128)(2,1)}), bf16[16,24,3072]{2,1,0:T(8,128)(2,1)}, u32[]{:S(2)}, u32[]{:S(2)}) async-start(bf16[16,24,3072]{2,1,0:T(8,128)(2,1)} %broadcast_in_dim.5), calls=%async_computation.1 | async-start | bytes 4718592 | tf_op jit(solution)/shard_map/all_to_all | solution.py:163
  64.8 135.1 %reduce-scatter.2.cloned.1.call-start = ((), (), s32[]{:S(2)}) async-start(), calls=%async_computation.5 | async-start | bytes 5570560 | tf_op jit(solution)/shard_map/reduce_scatter | solution.py:189
  66.2 37.0 %copy-start = (s32[20]{0:T(128)S(1)}, s32[20]{0:T(128)}, u32[]{:S(2)}) copy-start(s32[20]{0:T(128)} %down_index.3) | copy-start | bytes 244
  66.2 37.0 %copy-start.1 = (s32[20]{0:T(128)S(1)}, s32[20]{0:T(128)}, u32[]{:S(2)}) copy-start(s32[20]{0:T(128)} %up_index.1) | copy-start | bytes 244
  127.4 76.9 %all-to-all-start.2 = ((bf16[16,24,3072]{2,1,0:T(8,128)(2,1)}), bf16[16,24,3072]{2,1,0:T(8,128)(2,1)S(1)}, u32[]{:S(2)}, u32[]{:S(2)}) async-start(bf16[16,24,3072]{2,1,0:T(8,128)(2,1)} %bitcast.10), calls=%async_computation.2 | async-start | bytes 4718592 | tf_op jit(solution)/shard_map/all_to_all | solution.py:197
  199.9 8.3 %copy-start.3 = (bf16[640,256]{1,0:T(8,128)(2,1)S(1)}, bf16[640,256]{1,0:T(8,128)(2,1)}, u32[]{:S(2)}) copy-start(bf16[640,256]{1,0:T(8,128)(2,1)} %reduce-scatter.2.cloned.1.call-done) | copy-start | bytes 983044
  201.0 7.2 %collective-permute-start.1 = (bf16[40,8,256]{2,1,0:T(8,128)(2,1)S(1)}, bf16[40,8,256]{2,1,0:T(8,128)(2,1)S(1)}, u32[]{:S(2)}, u32[]{:S(2)}) collective-permute-start(bf16[40,8,256]{2,1,0:T(8,128)(2,1)S(1)} %broadcast_select_fusion), channel_id=1, source_target_pairs={{0,256},{16,272},{32,288},{48,304},{64,320},{80,336},{96,352},{112... | collective-permute-start | bytes 491528 | tf_op jit(solution)/shard_map/ppermute | solution.py:202
Sparse Core Ops, SparseCore 0:
  17.7 85.4 all-gather.1
  120.8 79.0 reduce-scatter.1

commit v2 on v1

v2 whole, which is shorter than its diff:
```python
import functools

import jax
import jax.numpy as jnp
from jax import lax
from jax.experimental import pallas as pl
from jax.experimental.pallas import tpu as pltpu
from jax.sharding import PartitionSpec as P

FF = 12288
GELU_C = 0.7978845608028654
VMEM_BYTES = 34 * 1024 * 1024
CHUNKS = 4


def bent_tanh(value):
    return jnp.tanh(GELU_C * (value + 0.044715 * value * value * value))


def gelu_slope(value, bent):
    return 0.5 * (1.0 + bent) + 0.5 * value * (1.0 - bent * bent) * GELU_C * (
        1.0 + 3.0 * 0.044715 * value * value
    )


def own_rows(wide, ring, kind):
    part = wide.shape[1] // 4
    columns = wide.shape[2]
    pieces = [
        wide[:, (2 * pair + kind) * part : (2 * pair + kind + 1) * part].reshape(ring * part, columns)
        for pair in range(2)
    ]
    return jnp.concatenate(pieces, axis=0).astype(jnp.bfloat16)


def sent_rows(up, down, ring):
    rows, columns = up.shape
    part = rows // (2 * ring)
    pieces = [
        block[pair * rows // 2 : (pair + 1) * rows // 2].reshape(ring, part, columns)
        for pair in range(2)
        for block in (up, down)
    ]
    return jnp.concatenate(pieces, axis=1).astype(jnp.bfloat16)


def span(number, block):
    return pl.ds(pl.multiple_of(number * block, block), block)


def place_down(index, count, slots, s, dense, per_row):
    ring, block = slots.shape[0], slots.shape[-1]

    @pl.when(s < count[0])
    def _():
        row, column = lax.div(index[s], per_row), lax.rem(index[s], per_row)
        wide = slots[:, s].astype(jnp.float32)
        dense[span(column, block), span(row, block)] = own_rows(wide, ring, 1)


def place_up(index, count, slots, s, dense, per_row):
    ring, block = slots.shape[0], slots.shape[-1]

    @pl.when(s < count[0])
    def _():
        row, column = lax.div(index[s], per_row), lax.rem(index[s], per_row)
        wide = slots[:, s].astype(jnp.float32)
        dense[span(row, block), span(column, block)] = own_rows(wide, ring, 0)


def terms_kernel(
    up_index, up_count, down_index, down_count, x_far, x_t_far, dy_far, slots, terms, hidden,
    held, x, x_t, dy, up, down, grad, hidden_t, arrived, left,
):
    ring, cap, both, block = slots.shape
    per_row = up.shape[1] // block
    chunk = cap // CHUNKS
    part_of = [pl.ds(i * chunk, chunk) for i in range(CHUNKS)]
    incoming = [
        pltpu.make_async_copy(slots.at[:, at], held.at[:, at], arrived.at[i]) for i, at in enumerate(part_of)
    ]
    outgoing = [
        pltpu.make_async_copy(held.at[:, at], terms.at[:, at], left.at[i]) for i, at in enumerate(part_of)
    ]
    operands = [
        pltpu.make_async_copy(far, near, arrived.at[CHUNKS + i])
        for i, (far, near) in enumerate(((x_far, x), (dy_far, dy), (x_t_far, x_t)))
    ]
    for copy in incoming + operands:
        copy.start()
    up[...] = jnp.zeros_like(up)
    down[...] = jnp.zeros_like(down)

    def place(s, _):
        place_up(up_index, up_count, held, s, up, per_row)
        place_down(down_index, down_count, held, s, down, per_row)
        return 0

    for i in range(CHUNKS):
        incoming[i].wait()
        lax.fori_loop(i * chunk, (i + 1) * chunk, place, 0)
    operands[0].wait()
    operands[1].wait()
    for column in range(per_row):
        part = slice(column * block, (column + 1) * block)
        pre = jnp.dot(x[...], up[:, part], preferred_element_type=jnp.float32)
        bent = bent_tanh(pre)
        unit = 0.5 * pre * (1.0 + bent)
        hidden[:, part] = unit.astype(jnp.bfloat16)
        hidden_t[part, :] = jnp.transpose(unit).astype(jnp.bfloat16)
        back = lax.dot_general(
            dy[...], down[part, :], (((1,), (1,)), ((), ())), preferred_element_type=jnp.float32
        )
        grad[column] = (back * gelu_slope(pre, bent)).astype(jnp.bfloat16)

    operands[2].wait()

    def term(s, _):
        row, column = lax.div(down_index[s], per_row), lax.rem(down_index[s], per_row)
        down_term = jnp.dot(
            hidden_t[span(column, block), :], dy[:, span(row, block)], preferred_element_type=jnp.float32
        ) * (s < down_count[0]).astype(jnp.float32)
        row, column = lax.div(up_index[s], per_row), lax.rem(up_index[s], per_row)
        up_term = jnp.dot(
            x_t[span(row, block), :], grad[column], preferred_element_type=jnp.float32
        ) * (s < up_count[0]).astype(jnp.float32)
        held[:, s] = sent_rows(up_term, down_term, ring)
        return 0

    for i in range(CHUNKS):
        lax.fori_loop(i * chunk, (i + 1) * chunk, term, 0, unroll=chunk)
        outgoing[i].start()
    for copy in outgoing:
        copy.wait()


def partial_kernel(down_index, down_count, hidden, slots, out, down):
    cap, block = slots.shape[1], slots.shape[3]
    per_row = hidden.shape[1] // block
    down[...] = jnp.zeros_like(down)

    def place(s, _):
        place_down(down_index, down_count, slots, s, down, per_row)
        return 0

    lax.fori_loop(0, cap, place, 0)
    step = 2 * block
    for at in range(0, out.shape[1], step):
        out[:, at : at + step] = jnp.dot(
            hidden[...], down[:, at : at + step], preferred_element_type=jnp.float32
        ).astype(jnp.bfloat16)


SCALARS = pl.BlockSpec(memory_space=pltpu.SMEM)
WHOLE = pl.BlockSpec(memory_space=pltpu.VMEM)
FAR = pl.BlockSpec(memory_space=pltpu.HBM)


def all_terms(up_index, up_count, down_index, down_count, x, x_t, dy, slots, units):
    rows, width = x.shape
    block = slots.shape[3]
    far = [pltpu.with_memory_space_constraint(value, pltpu.HBM) for value in (x, x_t, dy, slots)]
    flops = 2 * rows * width * units * 2 + 4 * rows * block * block * slots.shape[1]
    return pl.pallas_call(
        terms_kernel,
        out_shape=(
            pltpu.HBM(slots.shape, jnp.bfloat16),
            jax.ShapeDtypeStruct((rows, units), jnp.bfloat16),
        ),
        in_specs=[SCALARS] * 4 + [FAR] * 4,
        out_specs=(FAR, WHOLE),
        scratch_shapes=[
            pltpu.VMEM(slots.shape, jnp.bfloat16),
            pltpu.VMEM((rows, width), jnp.bfloat16),
            pltpu.VMEM((width, rows), jnp.bfloat16),
            pltpu.VMEM((rows, width), jnp.bfloat16),
            pltpu.VMEM((width, units), jnp.bfloat16),
            pltpu.VMEM((units, width), jnp.bfloat16),
            pltpu.VMEM((units // block, rows, block), jnp.bfloat16),
            pltpu.VMEM((units, rows), jnp.bfloat16),
            pltpu.SemaphoreType.DMA((CHUNKS + 3,)),
            pltpu.SemaphoreType.DMA((CHUNKS,)),
        ],
        compiler_params=pltpu.CompilerParams(vmem_limit_bytes=VMEM_BYTES),
        cost_estimate=pl.CostEstimate(flops=flops, bytes_accessed=4 * slots.size, transcendentals=rows * units),
        name="terms",
    )(up_index, up_count, down_index, down_count, *far)


def partial_sum(down_index, down_count, hidden, slots, width):
    rows, units = hidden.shape
    return pl.pallas_call(
        partial_kernel,
        out_shape=jax.ShapeDtypeStruct((rows, width), jnp.bfloat16),
        in_specs=[SCALARS] * 2 + [WHOLE] * 2,
        out_specs=WHOLE,
        scratch_shapes=[pltpu.VMEM((units, width), jnp.bfloat16)],
        compiler_params=pltpu.CompilerParams(vmem_limit_bytes=VMEM_BYTES),
        cost_estimate=pl.CostEstimate(
            flops=2 * rows * units * width, bytes_accessed=2 * slots.size, transcendentals=0
        ),
        name="partial",
    )(down_index, down_count, hidden, slots)


def spread(value, shards):
    copies = jnp.broadcast_to(value[None], (shards,) + value.shape)
    got = lax.all_to_all(copies, "tensor", split_axis=0, concat_axis=0, tiled=True)
    return got.reshape((shards * value.shape[0],) + value.shape[1:])


def side_by_side(first, left, right):
    both = jnp.where(first[None, :, None, None], left[:, None], right[:, None])
    return both.reshape(left.shape[0], 2 * left.shape[1], left.shape[2])


def body(tokens, cotangent, up_blocks, down_blocks, up_index, up_count, down_index, down_count):
    cap, part, block = up_blocks.shape
    groups = lax.axis_size("dp")
    shards = lax.axis_size("tensor")
    ring = groups // 2
    rings = [list(range(ring)), list(range(ring, groups))]
    across = [(i, (i + ring) % groups) for i in range(groups)]
    own = side_by_side(jnp.arange(2) == 0, up_blocks, down_blocks)
    other = lax.ppermute(own, "dp", across)
    upper = lax.axis_index("dp") >= ring
    pair = side_by_side((jnp.arange(2) == 1) == upper, own, other)
    slots = lax.all_gather(
        pair.reshape(cap * 4 * part, block), "dp", axis=0, tiled=True, axis_index_groups=rings
    ).reshape(ring, cap, 4 * part, block)
    x = spread(tokens, shards)
    dy = spread(cotangent, shards)
    rows, width = x.shape
    terms, hidden = all_terms(
        up_index, up_count, down_index, down_count, x, x.T, dy, slots, FF // shards
    )
    summed = lax.psum_scatter(
        terms.reshape(ring * cap * 4 * part, block),
        "dp",
        scatter_dimension=0,
        tiled=True,
        axis_index_groups=rings,
    ).reshape(cap, 4 * part, block)
    value = partial_sum(down_index, down_count, hidden, slots, width)
    got = lax.all_to_all(
        value.reshape(shards, rows // shards, width), "tensor", split_axis=0, concat_axis=0, tiled=True
    )
    mixed = jnp.sum(got.astype(jnp.float32), axis=0).astype(jnp.bfloat16)
    low, high = summed[:, : 2 * part], summed[:, 2 * part :]
    far = lax.ppermute(jnp.where(upper, low, high), "dp", across)
    grads = jnp.where(upper, high, low).astype(jnp.float32) + far.astype(jnp.float32)
    return (mixed, grads[:, :part], grads[:, part:])


def solution(mesh):
    in_specs = (
        P(("dp", "tensor"), None),
        P(("dp", "tensor"), None),
        P("tensor", "dp", None),
        P("tensor", "dp", None),
        P("tensor"),
        P("tensor"),
        P("tensor"),
        P("tensor"),
    )
    out_specs = (P(("dp", "tensor"), None), P("tensor", "dp", None), P("tensor", "dp", None))
    return jax.shard_map(body, mesh=mesh, in_specs=in_specs, out_specs=out_specs, check_vma=False)
```

time: 216 us -> 211 us (0.977)
  Pallas kernels: 24.1 us -> 18 us
    pallas_call x1, Pallas kernels: 17.4 us -> 13.1 us  [all_terms(): pl.pallas_call(terms_kernel, out_shape=(pltpu.HBM(slots.shape, jnp.bfloat...]
  transfers between devices with their start and end apart: 6 -> 6, of which waited for: 5 -> 5; matrix products, arithmetic and copies ran while one was open for 4% -> 4% of each run, Pallas kernels for 3% -> 2%
where the time goes in v2:
time: 211 us
  waiting for transfers between devices  106 us (50%)
  blocking collectives  37.4 us (18%)
  starting transfers between devices  21 us (10%)
  Pallas kernels  18 us (9%)
  between operations  15.5 us (7%)
  local copies, waits for them, and re-layouts  9.21 us (4%)
  other arithmetic  4.09 us (2%)
    reduce_scatter x1, waiting for transfers between devices, body(): lax.psum_scatter(terms.reshape(ring * cap * 4 * part, block), 'dp', scatt...  64.2 us
    all_to_all x1, blocking collectives, spread(): lax.all_to_all(copies, 'tensor', split_axis=0, concat_axis=0, tiled=True)  37.4 us
    all_to_all x1, waiting for transfers between devices, spread(): lax.all_to_all(copies, 'tensor', split_axis=0, concat_axis=0, tiled=True)  25.6 us
    pallas_call x1, Pallas kernels, all_terms(): pl.pallas_call(terms_kernel, out_shape=(pltpu.HBM(slots.shape, jnp.bfloat...  13.1 us
    all_gather x1, waiting for transfers between devices, body(): lax.all_gather(pair.reshape(cap * 4 * part, block), 'dp', axis=0, tiled=T...  8.9 us
    all_to_all x1, starting transfers between devices, body(): lax.all_to_all(value.reshape(shards, rows // shards, width), 'tensor', sp...  7.42 us
    all_to_all x1, starting transfers between devices, spread(): lax.all_to_all(copies, 'tensor', split_axis=0, concat_axis=0, tiled=True)  6.67 us
    pallas_call x1, Pallas kernels, partial_sum(): pl.pallas_call(partial_kernel, out_shape=jax.ShapeDtypeStruct((rows, widt...  4.84 us
  transfers between devices with their start and end apart: 6, of which 5 were waited for; matrix products, arithmetic and copies ran while one was open for 4% of the time, Pallas kernels for 2%

profile of v2, /device:TPU:6, one launch (start us, length us, event | category | flops | bytes accessed | tf_op | source)
XLA Modules:
  0.0 210.7 jit_solution(7230802592153854782)
XLA Ops:
  7.2 0.0 all-gather.2.cloned.1.call-start
  7.2 0.1 broadcast_in_dim.86
  7.3 0.1 broadcast_in_dim.87
  7.4 1.0 bitcast_select_fusion.1
  8.4 3.5 %collective-permute-start = (bf16[20,16,256]{2,1,0:T(8,128)(2,1)S(1)}, bf16[20,16,256]{2,1,0:T(8,128)(2,1)S(1)}, u32[]{:S(2)}, u32[]{:S(2)}) collective-permute-start(bf16[20,16,256]{2,1,0:T(8,128)(2,1)S(1)} %bitcast_select_fusion.1), channel_id=1, source_target_pairs={{0,256},{16,272},{32,288},{48,304},{64,320},{80,336},{96,352},{112... | collective-permute-start | bytes 491528 | tf_op jit(solution)/shard_map/ppermute | solution.py:225
  11.9 0.1 broadcast_in_dim.83
  12.0 0.1 broadcast_in_dim.84
  12.1 4.1 %collective-permute-done = bf16[20,16,256]{2,1,0:T(8,128)(2,1)S(1)} collective-permute-done((bf16[20,16,256]{2,1,0:T(8,128)(2,1)S(1)}, bf16[20,16,256]{2,1,0:T(8,128)(2,1)S(1)}, u32[]{:S(2)}, u32[]{:S(2)}) %collective-permute-start) | collective-permute-done | bytes 163872 | tf_op jit(solution)/shard_map/ppermute | solution.py:225
  16.2 0.9 bitcast_select_fusion
  17.1 0.0 all-gather.2.cloned.1.call-update
  17.1 1.2 broadcast_in_dim.81
  18.3 0.0 copy-start.5
  18.3 37.4 %all_to_all.15 = bf16[16,24,3072]{2,1,0:T(8,128)(2,1)S(1)} all-to-all(bf16[16,24,3072]{2,1,0:T(8,128)(2,1)S(1)} %broadcast_in_dim.81), channel_id=1, replica_groups=mesh['dp'=32,'tensor'=16] {'tensor'}, dimensions={0} | all-to-all | bytes 4718592 | tf_op jit(solution)/shard_map/all_to_all | solution.py:208
  55.7 0.0 copy-done.5
  55.7 0.0 copy-start.3
  55.7 2.0 broadcast_in_dim.82
  57.7 6.7 %all-to-all-start.1 = ((bf16[16,24,3072]{2,1,0:T(8,128)(2,1)}), bf16[16,24,3072]{2,1,0:T(8,128)(2,1)}, u32[]{:S(2)}, u32[]{:S(2)}) async-start(bf16[16,24,3072]{2,1,0:T(8,128)(2,1)} %broadcast_in_dim.82), calls=%async_computation.1 | async-start | bytes 4718592 | tf_op jit(solution)/shard_map/all_to_all | solution.py:208
  64.4 0.0 reduce-scatter.2.cloned.1.call-start
  65.7 0.0 copy-done.3
  65.7 0.0 copy-start.1
  65.7 0.0 copy-start.2
  65.7 2.5 %copy.13 = bf16[384,3072]{0,1:T(8,128)(2,1)} copy(bf16[384,3072]{1,0:T(8,128)(2,1)S(1)} %bitcast.17) | data formatting | bytes 4718592 | tf_op jit(solution)/shard_map/reshape | solution.py:209
  68.2 25.6 %all-to-all-done.1 = bf16[16,24,3072]{2,1,0:T(8,128)(2,1)} async-done(((bf16[16,24,3072]{2,1,0:T(8,128)(2,1)}), bf16[16,24,3072]{2,1,0:T(8,128)(2,1)}, u32[]{:S(2)}, u32[]{:S(2)}) %all-to-all-start.1) | async-done | bytes 2359328 | tf_op jit(solution)/shard_map/all_to_all | solution.py:208
  93.8 8.9 %all-gather.2.cloned.1.call-done = bf16[10240,256]{1,0:T(8,128)(2,1)} async-done(((bf16[640,256]{1,0:T(8,128)(2,1)}), bf16[10240,256]{1,0:T(8,128)(2,1)}) %all-gather.2.cloned.1.call-update) | async-done | bytes 5242896 | tf_op jit(solution)/shard_map/all_gather | solution.py:228
  102.7 0.0 copy-done.1
  102.7 0.0 copy-done.2
  102.8 13.1 %terms.1 = (bf16[16,20,32,256]{3,2,1,0:T(8,128)(2,1)}, bf16[384,768]{1,0:T(8,128)(2,1)S(1)}) custom-call(s32[20]{0:T(128)S(1)} %copy-done.2, s32[1]{0:T(128)S(6)} %copy.14.up_count, s32[20]{0:T(128)S(1)} %copy-done.1, s32[1]{0:T(128)S(6)} %copy.15.down_count, bf16[384,3072]{1,0:T(8,128)(2,1)} %bitcast.18, bf16[3072,384]{1,0:T(8,128)(2,1)} %bitcast.20, ...), custom_call_target="tpu_custom_call" | custom-call | flops 5637144576 | bytes 10485760 | tf_op jit(solution)/shard_map/terms/pallas_call | solution.py:164
  115.9 0.0 reduce-scatter.2.cloned.1.call-update
  115.9 0.0 copy-start
  115.9 2.5 %copy-done = bf16[10240,256]{1,0:T(8,128)(2,1)S(1)} copy-done((bf16[10240,256]{1,0:T(8,128)(2,1)S(1)}, bf16[10240,256]{1,0:T(8,128)(2,1)}, u32[]{:S(2)}) %copy-start) | copy-done | bytes 5242904
  118.4 4.8 %partial.1 = bf16[384,3072]{1,0:T(8,128)(2,1)} custom-call(s32[20]{0:T(128)S(1)} %copy-done.1, s32[1]{0:T(128)S(6)} %copy.15.down_count, bf16[384,768]{1,0:T(8,128)(2,1)S(1)} %get-tuple-element.5.hidden, bf16[16,20,32,256]{3,2,1,0:T(8,128)(2,1)S(1)} %bitcast.16), custom_call_target="tpu_custom_call" | custom-call | flops 1811939328 | bytes 5242880 | tf_op jit(solution)/shard_map/partial/pallas_call | solution.py:192
  123.2 7.4 %all-to-all-start.2 = ((bf16[16,24,3072]{2,1,0:T(8,128)(2,1)}), bf16[16,24,3072]{2,1,0:T(8,128)(2,1)S(1)}, u32[]{:S(2)}, u32[]{:S(2)}) async-start(bf16[16,24,3072]{2,1,0:T(8,128)(2,1)} %bitcast.8), calls=%async_computation.2 | async-start | bytes 4718592 | tf_op jit(solution)/shard_map/all_to_all | solution.py:245
  130.7 64.2 %reduce-scatter.2.cloned.1.call-done = bf16[640,256]{1,0:T(8,128)(2,1)} async-done(((bf16[10240,256]{1,0:T(8,128)(2,1)}), bf16[640,256]{1,0:T(8,128)(2,1)}) %reduce-scatter.2.cloned.1.call-update) | async-done | bytes 327696 | tf_op jit(solution)/shard_map/reduce_scatter | solution.py:237
  194.8 0.0 copy-start.4
  194.8 1.1 broadcast_select_fusion
  195.9 3.3 %collective-permute-start.1 = (bf16[20,16,256]{2,1,0:T(8,128)(2,1)S(1)}, bf16[20,16,256]{2,1,0:T(8,128)(2,1)S(1)}, u32[]{:S(2)}, u32[]{:S(2)}) collective-permute-start(bf16[20,16,256]{2,1,0:T(8,128)(2,1)S(1)} %broadcast_select_fusion), channel_id=1, source_target_pairs={{0,256},{16,272},{32,288},{48,304},{64,320},{80,336},{96,352},{112... | collective-permute-start | bytes 491528 | tf_op jit(solution)/shard_map/ppermute | solution.py:250
  199.2 0.0 all-to-all-done.2
  199.2 1.1 reduce_sum.12
  200.3 2.8 %collective-permute-done.1 = bf16[20,16,256]{2,1,0:T(8,128)(2,1)S(1)} collective-permute-done((bf16[20,16,256]{2,1,0:T(8,128)(2,1)S(1)}, bf16[20,16,256]{2,1,0:T(8,128)(2,1)S(1)}, u32[]{:S(2)}, u32[]{:S(2)}) %collective-permute-start.1) | collective-permute-done | bytes 163872 | tf_op jit(solution)/shard_map/ppermute | solution.py:250
  203.1 0.0 copy-done.4
  203.1 0.1 convert_add_fusion
  203.2 0.7 fusion
  (2 shorter events, 0.0 us)
Async XLA Ops:
  7.2 95.6 %all-gather.2.cloned.1.call-start = ((), (), s32[]{:S(2)}) async-start(), calls=%async_computation.4 | async-start | bytes 5570560 | tf_op jit(solution)/shard_map/all_gather | solution.py:228
  8.4 7.8 %collective-permute-start = (bf16[20,16,256]{2,1,0:T(8,128)(2,1)S(1)}, bf16[20,16,256]{2,1,0:T(8,128)(2,1)S(1)}, u32[]{:S(2)}, u32[]{:S(2)}) collective-permute-start(bf16[20,16,256]{2,1,0:T(8,128)(2,1)S(1)} %bitcast_select_fusion.1), channel_id=1, source_target_pairs={{0,256},{16,272},{32,288},{48,304},{64,320},{80,336},{96,352},{112... | collective-permute-start | bytes 491528 | tf_op jit(solution)/shard_map/ppermute | solution.py:225
  18.3 37.4 %copy-start.5 = (bf16[24,3072]{1,0:T(8,128)(2,1)S(1)}, bf16[24,3072]{1,0:T(8,128)(2,1)}, u32[]{:S(2)}) copy-start(bf16[24,3072]{1,0:T(8,128)(2,1)} %param.9) | copy-start | bytes 442372
  55.7 10.0 %copy-start.3 = (bf16[16,24,3072]{2,1,0:T(8,128)(2,1)}, bf16[16,24,3072]{2,1,0:T(8,128)(2,1)S(1)}, u32[]{:S(2)}) copy-start(bf16[16,24,3072]{2,1,0:T(8,128)(2,1)S(1)} %all_to_all.15) | copy-start | bytes 7077892
  57.7 36.2 %all-to-all-start.1 = ((bf16[16,24,3072]{2,1,0:T(8,128)(2,1)}), bf16[16,24,3072]{2,1,0:T(8,128)(2,1)}, u32[]{:S(2)}, u32[]{:S(2)}) async-start(bf16[16,24,3072]{2,1,0:T(8,128)(2,1)} %broadcast_in_dim.82), calls=%async_computation.1 | async-start | bytes 4718592 | tf_op jit(solution)/shard_map/all_to_all | solution.py:208
  64.4 130.5 %reduce-scatter.2.cloned.1.call-start = ((), (), s32[]{:S(2)}) async-start(), calls=%async_computation.5 | async-start | bytes 5570560 | tf_op jit(solution)/shard_map/reduce_scatter | solution.py:237
  65.7 37.0 %copy-start.1 = (s32[20]{0:T(128)S(1)}, s32[20]{0:T(128)}, u32[]{:S(2)}) copy-start(s32[20]{0:T(128)} %down_index.3) | copy-start | bytes 244
  65.7 37.0 %copy-start.2 = (s32[20]{0:T(128)S(1)}, s32[20]{0:T(128)}, u32[]{:S(2)}) copy-start(s32[20]{0:T(128)} %up_index.1) | copy-start | bytes 244
  115.9 2.5 %copy-start = (bf16[10240,256]{1,0:T(8,128)(2,1)S(1)}, bf16[10240,256]{1,0:T(8,128)(2,1)}, u32[]{:S(2)}) copy-start(bf16[10240,256]{1,0:T(8,128)(2,1)} %all-gather.2.cloned.1.call-done) | copy-start | bytes 15728644
  123.2 76.0 %all-to-all-start.2 = ((bf16[16,24,3072]{2,1,0:T(8,128)(2,1)}), bf16[16,24,3072]{2,1,0:T(8,128)(2,1)S(1)}, u32[]{:S(2)}, u32[]{:S(2)}) async-start(bf16[16,24,3072]{2,1,0:T(8,128)(2,1)} %bitcast.8), calls=%async_computation.2 | async-start | bytes 4718592 | tf_op jit(solution)/shard_map/all_to_all | solution.py:245
  194.8 8.3 %copy-start.4 = (bf16[640,256]{1,0:T(8,128)(2,1)S(1)}, bf16[640,256]{1,0:T(8,128)(2,1)}, u32[]{:S(2)}) copy-start(bf16[640,256]{1,0:T(8,128)(2,1)} %reduce-scatter.2.cloned.1.call-done) | copy-start | bytes 983044
  195.9 7.2 %collective-permute-start.1 = (bf16[20,16,256]{2,1,0:T(8,128)(2,1)S(1)}, bf16[20,16,256]{2,1,0:T(8,128)(2,1)S(1)}, u32[]{:S(2)}, u32[]{:S(2)}) collective-permute-start(bf16[20,16,256]{2,1,0:T(8,128)(2,1)S(1)} %broadcast_select_fusion), channel_id=1, source_target_pairs={{0,256},{16,272},{32,288},{48,304},{64,320},{80,336},{96,352},{112... | collective-permute-start | bytes 491528 | tf_op jit(solution)/shard_map/ppermute | solution.py:250
Sparse Core Ops, SparseCore 0:
  17.3 85.4 all-gather.1
  116.0 78.7 reduce-scatter.1

commit v3 on v2

v3 whole, which is shorter than its diff:
```python
import jax
import jax.numpy as jnp
from jax import lax
from jax.experimental import pallas as pl
from jax.experimental.pallas import tpu as pltpu
from jax.sharding import Mesh
from jax.sharding import PartitionSpec as P

FF = 12288
GELU_C = 0.7978845608028654
VMEM_BYTES = 36 * 1024 * 1024
CHUNKS = 4
PAIR, RING, PLANE, CORE = "y_lo", "z", "yx", "core"
SCALARS = pl.BlockSpec(memory_space=pltpu.SMEM)
WHOLE = pl.BlockSpec(memory_space=pltpu.VMEM)
FAR = pl.BlockSpec(memory_space=pltpu.HBM)


def bent_tanh(value):
    return jnp.tanh(GELU_C * (value + 0.044715 * value * value * value))


def gelu_slope(value, bent):
    return 0.5 * (1.0 + bent) + 0.5 * value * (1.0 - bent * bent) * GELU_C * (
        1.0 + 3.0 * 0.044715 * value * value
    )


def quarter(wide, number):
    ring, rows, half = wide.shape
    part = rows // 4
    return wide[:, number * part : (number + 1) * part].reshape(ring * part, half)


def up_half(wide):
    return jnp.concatenate([quarter(wide, 0), quarter(wide, 1)], axis=0).astype(jnp.bfloat16)


def down_half(wide):
    return jnp.concatenate([quarter(wide, 2), quarter(wide, 3)], axis=1).astype(jnp.bfloat16)


def sent_rows(up, down, ring):
    half = up.shape[1]
    pieces = [up[:half], up[half:], down[:, :half], down[:, half:]]
    pieces = [piece.reshape(ring, half // ring, half) for piece in pieces]
    return jnp.concatenate(pieces, axis=1).astype(jnp.bfloat16)


def span(number, size):
    return pl.ds(pl.multiple_of(number * size, size), size)


def place_up(index, count, slots, s, dense, per_row):
    half = slots.shape[3]

    @pl.when(s < count[0])
    def _():
        row, column = lax.div(index[s], per_row), lax.rem(index[s], per_row)
        dense[span(row, 2 * half), span(column, half)] = up_half(slots[:, s].astype(jnp.float32))


def place_down(index, count, slots, s, dense, per_row):
    half = slots.shape[3]

    @pl.when(s < count[0])
    def _():
        row, column = lax.div(index[s], per_row), lax.rem(index[s], per_row)
        dense[span(column, half), span(row, 2 * half)] = down_half(slots[:, s].astype(jnp.float32))


def terms_kernel(
    up_index, up_count, down_index, down_count, core, mine, other, slots, terms, hidden,
    held, x, dy, x_t, up, down, grad, hidden_t, arrived, left,
):
    ring, cap, _, half = slots.shape
    per_row = up.shape[1] // half
    rows, width = x.shape
    chunk = cap // CHUNKS
    part_of = [pl.ds(i * chunk, chunk) for i in range(CHUNKS)]
    incoming = [
        pltpu.make_async_copy(slots.at[:, at], held.at[:, at], arrived.at[i]) for i, at in enumerate(part_of)
    ]
    outgoing = [
        pltpu.make_async_copy(held.at[:, at], terms.at[:, at], left.at[i]) for i, at in enumerate(part_of)
    ]
    straight = [
        pltpu.make_async_copy(mine, x, arrived.at[CHUNKS]),
        pltpu.make_async_copy(other, dy, arrived.at[CHUNKS + 1]),
    ]
    crossed = [
        pltpu.make_async_copy(other, x, arrived.at[CHUNKS]),
        pltpu.make_async_copy(mine, dy, arrived.at[CHUNKS + 1]),
    ]
    for copy in incoming:
        copy.start()

    @pl.when(core[0] == 0)
    def _():
        for copy in straight:
            copy.start()

    @pl.when(core[0] != 0)
    def _():
        for copy in crossed:
            copy.start()

    up[...] = jnp.zeros_like(up)
    down[...] = jnp.zeros_like(down)

    def place(s, _):
        place_up(up_index, up_count, held, s, up, per_row)
        place_down(down_index, down_count, held, s, down, per_row)
        return 0

    for i in range(CHUNKS):
        incoming[i].wait()
        lax.fori_loop(i * chunk, (i + 1) * chunk, place, 0)

    @pl.when(core[0] == 0)
    def _():
        for copy in straight:
            copy.wait()

    @pl.when(core[0] != 0)
    def _():
        for copy in crossed:
            copy.wait()

    for at in range(0, rows, rows // 2):
        part = slice(at, at + rows // 2)
        pre = jnp.dot(x[part, :], up[...], preferred_element_type=jnp.float32)
        bent = bent_tanh(pre)
        unit = 0.5 * pre * (1.0 + bent)
        hidden[part, :] = unit.astype(jnp.bfloat16)
        hidden_t[:, part] = jnp.transpose(unit).astype(jnp.bfloat16)
        back = lax.dot_general(
            dy[part, :], down[...], (((1,), (1,)), ((), ())), preferred_element_type=jnp.float32
        )
        grad[part, :] = (back * gelu_slope(pre, bent)).astype(jnp.bfloat16)
    for at in range(0, width, 2 * half):
        x_t[at : at + 2 * half, :] = jnp.transpose(x[:, at : at + 2 * half])

    def term(s, _):
        row, column = lax.div(down_index[s], per_row), lax.rem(down_index[s], per_row)
        down_term = jnp.dot(
            hidden_t[span(column, half), :], dy[:, span(row, 2 * half)], preferred_element_type=jnp.float32
        ) * (s < down_count[0]).astype(jnp.float32)
        row, column = lax.div(up_index[s], per_row), lax.rem(up_index[s], per_row)
        up_term = jnp.dot(
            x_t[span(row, 2 * half), :], grad[:, span(column, half)], preferred_element_type=jnp.float32
        ) * (s < up_count[0]).astype(jnp.float32)
        held[:, s] = sent_rows(up_term, down_term, ring)
        return 0

    for i in range(CHUNKS):
        lax.fori_loop(i * chunk, (i + 1) * chunk, term, 0, unroll=chunk)
        outgoing[i].start()
    for copy in outgoing:
        copy.wait()


def partial_kernel(down_index, down_count, hidden, slots, out, down):
    cap, half = slots.shape[1], slots.shape[3]
    per_row = hidden.shape[1] // half
    down[...] = jnp.zeros_like(down)

    def place(s, _):
        place_down(down_index, down_count, slots, s, down, per_row)
        return 0

    lax.fori_loop(0, cap, place, 0)
    step = 4 * half
    for at in range(0, out.shape[1], step):
        out[:, at : at + step] = jnp.dot(
            hidden[...], down[:, at : at + step], preferred_element_type=jnp.float32
        ).astype(jnp.bfloat16)


def all_terms(up_index, up_count, down_index, down_count, core, mine, other, slots, units):
    rows, width = mine.shape
    flops = 4 * rows * width * units + 2 * rows * slots.size
    mine, other, slots = (pltpu.with_memory_space_constraint(v, pltpu.HBM) for v in (mine, other, slots))
    return pl.pallas_call(
        terms_kernel,
        out_shape=(
            pltpu.HBM(slots.shape, jnp.bfloat16),
            jax.ShapeDtypeStruct((rows, units), jnp.bfloat16),
        ),
        in_specs=[SCALARS] * 5 + [FAR] * 3,
        out_specs=(FAR, WHOLE),
        scratch_shapes=[
            pltpu.VMEM(slots.shape, jnp.bfloat16),
            pltpu.VMEM((rows, width), jnp.bfloat16),
            pltpu.VMEM((rows, width), jnp.bfloat16),
            pltpu.VMEM((width, rows), jnp.bfloat16),
            pltpu.VMEM((width, units), jnp.bfloat16),
            pltpu.VMEM((units, width), jnp.bfloat16),
            pltpu.VMEM((rows, units), jnp.bfloat16),
            pltpu.VMEM((units, rows), jnp.bfloat16),
            pltpu.SemaphoreType.DMA((CHUNKS + 2,)),
            pltpu.SemaphoreType.DMA((CHUNKS,)),
        ],
        compiler_params=pltpu.CompilerParams(vmem_limit_bytes=VMEM_BYTES),
        cost_estimate=pl.CostEstimate(flops=flops, bytes_accessed=4 * slots.size, transcendentals=rows * units),
        name="terms",
    )(up_index, up_count, down_index, down_count, core, mine, other, slots)


def partial_sum(down_index, down_count, hidden, slots, width):
    rows, units = hidden.shape
    return pl.pallas_call(
        partial_kernel,
        out_shape=pltpu.HBM((rows, width), jnp.bfloat16),
        in_specs=[SCALARS] * 2 + [WHOLE] * 2,
        out_specs=WHOLE,
        scratch_shapes=[pltpu.VMEM((units, width), jnp.bfloat16)],
        compiler_params=pltpu.CompilerParams(vmem_limit_bytes=VMEM_BYTES),
        cost_estimate=pl.CostEstimate(
            flops=2 * rows * units * width, bytes_accessed=2 * slots.size, transcendentals=0
        ),
        name="partial",
    )(down_index, down_count, hidden, slots)


def swapped(value, axis):
    return lax.ppermute(value, axis, [(0, 1), (1, 0)])


def body(tokens, cotangent, up_blocks, down_blocks, up_index, up_count, down_index, down_count):
    cap, part, block = up_blocks.shape
    ring = lax.axis_size(RING)
    shards = lax.axis_size(PLANE) * lax.axis_size(CORE)
    half = block // 2
    second = lax.axis_index(PAIR) == 1
    core = lax.axis_index(CORE)
    left, right = up_blocks[:, :, :half], up_blocks[:, :, half:]
    far = swapped(jnp.where(second, left, right), PAIR)
    near = jnp.where(second, right, left)
    rows, width = tokens.shape
    members = 2 * shards
    both = jnp.broadcast_to(jnp.stack([tokens, cotangent])[None], (shards, 2, rows, width))
    number = jnp.arange(4)[None, :, None, None]
    quarters = jnp.where(
        number < 2,
        jnp.where((number == 1) == second, near[:, None], far[:, None]),
        jnp.where(number == 2, down_blocks[:, None, :, :half], down_blocks[:, None, :, half:]),
    )
    slots = lax.all_gather(quarters.reshape(cap * 4 * part, half), RING, axis=0, tiled=True)
    slots = slots.reshape(ring, cap, 4 * part, half)
    mine = lax.cond(
        up_count[0] > 0,
        lambda value: lax.all_to_all(value, (PAIR, PLANE, CORE), split_axis=0, concat_axis=0, tiled=True),
        lambda value: value,
        both.reshape(members, rows, width),
    ).reshape(members * rows, width)
    other = swapped(mine, CORE)
    terms, hidden = all_terms(
        up_index, up_count, down_index, down_count, core.reshape(1), mine, other, slots, FF // members
    )
    summed = lax.psum_scatter(
        terms.reshape(ring * cap * 4 * part, half), RING, scatter_dimension=0, tiled=True
    ).reshape(cap, 4 * part, half)
    value = partial_sum(down_index, down_count, hidden, slots, width).reshape(members, rows, width)
    got = lax.all_to_all(value, (PAIR, PLANE, CORE), split_axis=0, concat_axis=0, tiled=True)
    mixed = jnp.sum(got.astype(jnp.float32), axis=0).astype(jnp.bfloat16)
    low, high = summed[:, :part], summed[:, part : 2 * part]
    far = swapped(jnp.where(second, low, high), PAIR)
    near = jnp.where(second, high, low)
    up_grad = jnp.concatenate([jnp.where(second, far, near), jnp.where(second, near, far)], axis=2)
    down_grad = jnp.concatenate([summed[:, 2 * part : 3 * part], summed[:, 3 * part :]], axis=2)
    return (mixed, up_grad.astype(jnp.float32), down_grad.astype(jnp.float32))


def solution(mesh):
    shape = mesh.devices.shape
    split = Mesh(mesh.devices.reshape(2, shape[0] // 2, shape[1] // 2, 2), (PAIR, RING, PLANE, CORE))
    by_rows = P((PAIR, RING, PLANE, CORE), None)
    by_blocks = P((PLANE, CORE), (PAIR, RING), None)
    by_shard = P((PLANE, CORE))
    return jax.shard_map(
        body,
        mesh=split,
        in_specs=(by_rows, by_rows, by_blocks, by_blocks, by_shard, by_shard, by_shard, by_shard),
        out_specs=(by_rows, by_blocks, by_blocks),
        check_vma=False,
    )
```

time: 211 us -> 199 us (0.943); the launches traced: 211 us -> 197 us
  waiting for transfers between devices: 106 us -> 13.5 us
  blocking collectives: 37.4 us -> 126 us
  starting transfers between devices: 21 us -> 8.85 us
  local copies, waits for them, and re-layouts: 9.21 us -> 1.94 us
  other arithmetic: 4.09 us -> 9.78 us
  Pallas kernels: 18 us -> 21 us
    all_to_all x1 -> x2, blocking collectives: 37.4 us -> 126 us  [body(): lax.all_to_all(value, (PAIR, PLANE, CORE), split_axis=0, concat_axis=0, t...]
    reduce_scatter x1, waiting for transfers between devices: 64.2 us -> 0.01 us  [body(): lax.psum_scatter(terms.reshape(ring * cap * 4 * part, half), RING, scatte...]
    all_to_all x2 -> x0, waiting for transfers between devices: 25.6 us -> none  [the longest x1 25.6 us: spread(): lax.all_to_all(copies, 'tensor', split_axis=0, concat_axis=0, tiled=True)]
    all_to_all x2 -> x0, starting transfers between devices: 14.1 us -> none  [the longest x1 7.42 us: body(): lax.all_to_all(value.reshape(shards, rows // shards, width), 'tensor', sp...]
    all_gather x1, waiting for transfers between devices: 8.9 us -> 3.66 us  [body(): lax.all_gather(quarters.reshape(cap * 4 * part, half), RING, axis=0, tile...]
    reduce_sum x1, other arithmetic: 1.06 us -> 3.92 us  [body(): mixed = jnp.sum(got.astype(jnp.float32), axis=0).astype(jnp.bfloat16)]
    ppermute x2 -> x3, waiting for transfers between devices: 6.95 us -> 9.76 us  [swapped(): return lax.ppermute(value, axis, [(0, 1), (1, 0)])]
    reshape x1 -> x0, local copies, waits for them, and re-layouts: 2.5 us -> none  [spread(): return got.reshape((shards * value.shape[0],) + value.shape[1:])]
  transfers between devices with their start and end apart: 6 -> 5, of which waited for: 5 -> 4; matrix products, arithmetic and copies ran while one was open for 4% -> 4% of each run, Pallas kernels for 2% -> 3%
where the time goes in v3:
time: 199 us; the launch traced here: 197 us
  blocking collectives  126 us (63%)
  Pallas kernels  21 us (11%)
  between operations  15.4 us (8%)
  waiting for transfers between devices  13.5 us (7%)
  other arithmetic  9.78 us (5%)
  starting transfers between devices  8.85 us (4%)
    all_to_all x2, blocking collectives, body(): lax.all_to_all(value, (PAIR, PLANE, CORE), split_axis=0, concat_axis=0, t...  126 us
    pallas_call x1, Pallas kernels, all_terms(): pl.pallas_call(terms_kernel, out_shape=(pltpu.HBM(slots.shape, jnp.bfloat...  15 us
    ppermute x3, waiting for transfers between devices, swapped(): return lax.ppermute(value, axis, [(0, 1), (1, 0)])  9.76 us
    ppermute x3, starting transfers between devices, swapped(): return lax.ppermute(value, axis, [(0, 1), (1, 0)])  8.78 us
    pallas_call x1, Pallas kernels, partial_sum(): pl.pallas_call(partial_kernel, out_shape=pltpu.HBM((rows, width), jnp.bfl...  5.95 us
  transfers between devices with their start and end apart: 5, of which 4 were waited for; matrix products, arithmetic and copies ran while one was open for 4% of the time, Pallas kernels for 3%

profile of v3, /device:TPU:6, one launch (start us, length us, event | category | flops | bytes accessed | tf_op | source)
XLA Modules:
  0.0 196.6 jit_solution(4323894658089712254)
XLA Ops:
  7.2 0.0 all-gather.2.cloned.1.call-start
  7.2 0.8 broadcast_select_fusion.5
  8.0 3.5 %collective-permute-start.1 = (bf16[20,8,128]{2,1,0:T(8,128)(2,1)S(1)}, bf16[20,8,128]{2,1,0:T(8,128)(2,1)S(1)}, u32[]{:S(2)}, u32[]{:S(2)}) collective-permute-start(bf16[20,8,128]{2,1,0:T(8,128)(2,1)S(1)} %get-tuple-element.24), channel_id=1, source_target_pairs={{0,256},{256,0},{1,257},{257,1},{2,258},{258,2},{3,259},{259,3},{4... | collective-permute-start | bytes 122888 | tf_op jit(solution)/shard_map/ppermute | solution.py:227
  11.5 0.8 fusion.2
  13.0 0.1 broadcast_in_dim.92
  13.1 0.1 broadcast_in_dim.93
  13.2 0.1 broadcast_in_dim.82
  13.3 0.1 broadcast_in_dim.83
  13.4 0.1 broadcast_in_dim.85
  13.5 0.1 broadcast_in_dim.86
  13.6 0.4 collective-permute-done.1
  13.9 1.0 fusion
  14.9 0.0 all-gather.2.cloned.1.call-update
  14.9 0.0 reduce-scatter.2.cloned.1.call-start
  15.0 1.0 pad_maximum_fusion
  16.0 0.0 copy-start.1
  16.0 0.0 copy-start.2
  16.0 64.5 %conditional.1 = (bf16[768,3072]{1,0:T(8,128)(2,1)}) conditional(s32[]{:T(128)} %bitcast.4, bf16[2,24,3072]{2,1,0:T(8,128)(2,1)S(1)} %pad_maximum_fusion, bf16[2,24,3072]{2,1,0:T(8,128)(2,1)S(1)} %pad_maximum_fusion), branch_computations={%region_0.1_spmd, %region_1.2_spmd} | conditional | bytes 14450696 | solution.py:251
  16.0 0.6 broadcast_in_dim.64
  16.6 63.9 %all_to_all.9 = bf16[32,24,3072]{2,1,0:T(8,128)(2,1)} all-to-all(bf16[32,24,3072]{2,1,0:T(8,128)(2,1)S(1)} %bitcast.26), channel_id=1, replica_groups=mesh['y_lo'=2,'z'=16,'yx'=8,'core'=2] {'y_lo','yx','core'}, dimensions={0} | all-to-all | bytes 9437184 | tf_op jit(solution)/shard_map/cond/branch_1_fun/all_to_all | solution.py:253
  80.5 2.3 %collective-permute-start = (bf16[768,3072]{1,0:T(8,128)(2,1)}, bf16[768,3072]{1,0:T(8,128)(2,1)}, u32[]{:S(2)}, u32[]{:S(2)}) collective-permute-start(bf16[768,3072]{1,0:T(8,128)(2,1)} %get-tuple-element.27.mine), channel_id=1, source_target_pairs={{0,1},{1,0},{2,3},{3,2},{4,5},{5,4},{6,7},{7,6},{8,9},{9,8},{10,11... | collective-permute-start | bytes 14155784 | tf_op jit(solution)/shard_map/ppermute | solution.py:227
  83.5 7.2 %collective-permute-done.other = bf16[768,3072]{1,0:T(8,128)(2,1)} collective-permute-done((bf16[768,3072]{1,0:T(8,128)(2,1)}, bf16[768,3072]{1,0:T(8,128)(2,1)}, u32[]{:S(2)}, u32[]{:S(2)}) %collective-permute-start) | collective-permute-done | bytes 4718624 | tf_op jit(solution)/shard_map/ppermute | solution.py:227
  90.7 3.7 %all-gather.2.cloned.1.call-done = bf16[10240,128]{1,0:T(8,128)(2,1)} async-done(((bf16[640,128]{1,0:T(8,128)(2,1)}), bf16[10240,128]{1,0:T(8,128)(2,1)}) %all-gather.2.cloned.1.call-update) | async-done | bytes 2621456 | tf_op jit(solution)/shard_map/all_gather | solution.py:249
  94.3 0.0 copy-done.1
  94.3 0.0 copy-done.2
  94.3 0.0 copy-start
  94.3 15.0 %terms.1 = (bf16[16,20,32,128]{3,2,1,0:T(8,128)(2,1)}, bf16[768,384]{1,0:T(8,128)(2,1)S(1)}) custom-call(s32[20]{0:T(128)S(1)} %copy-done.2, s32[1]{0:T(128)S(6)} %copy.13.up_count, s32[20]{0:T(128)S(1)} %copy-done.1, s32[1]{0:T(128)S(6)} %copy.14.down_count, s32[1]{0:T(128)} %bitcast.3.core, bf16[768,3072]{1,0:T(8,128)(2,1)} %get-tuple-element.27.mine, ...), custom_call_target="tpu_custom_call" | custom-call | flops 5637144576 | bytes 5242880 | tf_op jit(solution)/shard_map/terms/pallas_call | solution.py:184
  109.4 0.0 reduce-scatter.2.cloned.1.call-update
  109.4 0.0 copy-done
  109.4 6.0 %partial.1 = bf16[768,3072]{1,0:T(8,128)(2,1)} custom-call(s32[20]{0:T(128)S(1)} %copy-done.1, s32[1]{0:T(128)S(6)} %copy.14.down_count, bf16[768,384]{1,0:T(8,128)(2,1)S(1)} %get-tuple-element.16.hidden, bf16[16,20,32,128]{3,2,1,0:T(8,128)(2,1)S(1)} %bitcast.24), custom_call_target="tpu_custom_call" | custom-call | flops 1811939328 | bytes 2621440 | tf_op jit(solution)/shard_map/partial/pallas_call | solution.py:212
  115.4 62.2 %all_to_all.10 = bf16[32,24,3072]{2,1,0:T(8,128)(2,1)} all-to-all(bf16[32,24,3072]{2,1,0:T(8,128)(2,1)} %bitcast.25), channel_id=1, replica_groups=mesh['y_lo'=2,'z'=16,'yx'=8,'core'=2] {'y_lo','yx','core'}, dimensions={0} | all-to-all | bytes 9437184 | tf_op jit(solution)/shard_map/all_to_all | solution.py:265
  177.6 3.9 %reduce_sum.12 = bf16[24,3072]{1,0:T(8,128)(2,1)} reduce(bf16[32,24,3072]{2,1,0:T(8,128)(2,1)} %all_to_all.10, bf16[]{:T(256)} %constant.18.clone.1), dimensions={0}, to_apply=%region_2.3 | reduce | flops 2285568 | bytes 4866050 | tf_op jit(solution)/shard_map/reduce_sum | solution.py:266
  181.5 0.0 reduce-scatter.2.cloned.1.call-done
  181.5 0.9 fusion.1
  182.4 3.0 %collective-permute-start.2 = (bf16[20,8,128]{2,1,0:T(8,128)(2,1)S(1)}, bf16[20,8,128]{2,1,0:T(8,128)(2,1)S(1)}, u32[]{:S(2)}, u32[]{:S(2)}) collective-permute-start(bf16[20,8,128]{2,1,0:T(8,128)(2,1)S(1)} %get-tuple-element.22), channel_id=1, source_target_pairs={{0,256},{256,0},{1,257},{257,1},{2,258},{258,2},{3,259},{259,3},{4... | collective-permute-start | bytes 122888 | tf_op jit(solution)/shard_map/ppermute | solution.py:227
  185.4 0.7 maximum_convert_fusion.1
  186.1 2.2 %collective-permute-done.2 = bf16[20,8,128]{2,1,0:T(8,128)(2,1)S(1)} collective-permute-done((bf16[20,8,128]{2,1,0:T(8,128)(2,1)S(1)}, bf16[20,8,128]{2,1,0:T(8,128)(2,1)S(1)}, u32[]{:S(2)}, u32[]{:S(2)}) %collective-permute-start.2) | collective-permute-done | bytes 40992 | tf_op jit(solution)/shard_map/ppermute | solution.py:227
  188.3 0.8 broadcast_select_fusion.1
  189.1 0.7 maximum_convert_fusion
  (3 shorter events, 0.0 us)
Async XLA Ops:
  7.2 87.2 %all-gather.2.cloned.1.call-start = ((), (), s32[]{:S(2)}) async-start(), calls=%async_computation.3 | async-start | bytes 2785280 | tf_op jit(solution)/shard_map/all_gather | solution.py:249
  8.0 5.9 %collective-permute-start.1 = (bf16[20,8,128]{2,1,0:T(8,128)(2,1)S(1)}, bf16[20,8,128]{2,1,0:T(8,128)(2,1)S(1)}, u32[]{:S(2)}, u32[]{:S(2)}) collective-permute-start(bf16[20,8,128]{2,1,0:T(8,128)(2,1)S(1)} %get-tuple-element.24), channel_id=1, source_target_pairs={{0,256},{256,0},{1,257},{257,1},{2,258},{258,2},{3,259},{259,3},{4... | collective-permute-start | bytes 122888 | tf_op jit(solution)/shard_map/ppermute | solution.py:227
  14.9 166.6 %reduce-scatter.2.cloned.1.call-start = ((), (), s32[]{:S(2)}) async-start(), calls=%async_computation.4 | async-start | bytes 2785280 | tf_op jit(solution)/shard_map/reduce_scatter | solution.py:261
  16.0 78.3 %copy-start.1 = (s32[20]{0:T(128)S(1)}, s32[20]{0:T(128)}, u32[]{:S(2)}) copy-start(s32[20]{0:T(128)} %down_index.3) | copy-start | bytes 244
  16.0 78.3 %copy-start.2 = (s32[20]{0:T(128)S(1)}, s32[20]{0:T(128)}, u32[]{:S(2)}) copy-start(s32[20]{0:T(128)} %up_index.1) | copy-start | bytes 244
  80.5 10.1 %collective-permute-start = (bf16[768,3072]{1,0:T(8,128)(2,1)}, bf16[768,3072]{1,0:T(8,128)(2,1)}, u32[]{:S(2)}, u32[]{:S(2)}) collective-permute-start(bf16[768,3072]{1,0:T(8,128)(2,1)} %get-tuple-element.27.mine), channel_id=1, source_target_pairs={{0,1},{1,0},{2,3},{3,2},{4,5},{5,4},{6,7},{7,6},{8,9},{9,8},{10,11... | collective-permute-start | bytes 14155784 | tf_op jit(solution)/shard_map/ppermute | solution.py:227
  94.3 15.1 %copy-start = (bf16[10240,128]{1,0:T(8,128)(2,1)S(1)}, bf16[10240,128]{1,0:T(8,128)(2,1)}, u32[]{:S(2)}) copy-start(bf16[10240,128]{1,0:T(8,128)(2,1)} %all-gather.2.cloned.1.call-done) | copy-start | bytes 7864324
  182.4 5.9 %collective-permute-start.2 = (bf16[20,8,128]{2,1,0:T(8,128)(2,1)S(1)}, bf16[20,8,128]{2,1,0:T(8,128)(2,1)S(1)}, u32[]{:S(2)}, u32[]{:S(2)}) collective-permute-start(bf16[20,8,128]{2,1,0:T(8,128)(2,1)S(1)} %get-tuple-element.22), channel_id=1, source_target_pairs={{0,256},{256,0},{1,257},{257,1},{2,258},{258,2},{3,259},{259,3},{4... | collective-permute-start | bytes 122888 | tf_op jit(solution)/shard_map/ppermute | solution.py:227
Sparse Core Ops, SparseCore 0:
  15.1 79.2 all-gather.1
  109.5 71.4 reduce-scatter.1

commit v4 on v3

--- a/solution.py
+++ b/solution.py
@@ -10,6 +10,7 @@
 GELU_C = 0.7978845608028654
 VMEM_BYTES = 36 * 1024 * 1024
 CHUNKS = 4
+STEPS = 2
 PAIR, RING, PLANE, CORE = "y_lo", "z", "yx", "core"
 SCALARS = pl.BlockSpec(memory_space=pltpu.SMEM)
 WHOLE = pl.BlockSpec(memory_space=pltpu.VMEM)
@@ -84,29 +85,33 @@
     outgoing = [
         pltpu.make_async_copy(held.at[:, at], terms.at[:, at], left.at[i]) for i, at in enumerate(part_of)
     ]
-    straight = [
-        pltpu.make_async_copy(mine, x, arrived.at[CHUNKS]),
-        pltpu.make_async_copy(other, dy, arrived.at[CHUNKS + 1]),
-    ]
-    crossed = [
-        pltpu.make_async_copy(other, x, arrived.at[CHUNKS]),
-        pltpu.make_async_copy(mine, dy, arrived.at[CHUNKS + 1]),
-    ]
+    steps = [pl.ds(i * rows // STEPS, rows // STEPS) for i in range(STEPS)]
+
+    def operands(first, second, i):
+        at = steps[i]
+        return (
+            pltpu.make_async_copy(first.at[at], x.at[at], arrived.at[CHUNKS + 2 * i]),
+            pltpu.make_async_copy(second.at[at], dy.at[at], arrived.at[CHUNKS + 2 * i + 1]),
+        )
+
+    def on_operands(act, i):
+        @pl.when(core[0] == 0)
+        def _():
+            for copy in operands(mine, other, i):
+                act(copy)
+
+        @pl.when(core[0] != 0)
+        def _():
+            for copy in operands(other, mine, i):
+                act(copy)
+
     for copy in incoming:
         copy.start()
-
-    @pl.when(core[0] == 0)
-    def _():
-        for copy in straight:
-            copy.start()
-
-    @pl.when(core[0] != 0)
-    def _():
-        for copy in crossed:
-            copy.start()
-
+    on_operands(lambda copy: copy.start(), 0)
     up[...] = jnp.zeros_like(up)
     down[...] = jnp.zeros_like(down)
+    for i in range(1, STEPS):
+        on_operands(lambda copy: copy.start(), i)
 
     def place(s, _):
         place_up(up_index, up_count, held, s, up, per_row)
@@ -117,18 +122,8 @@
         incoming[i].wait()
         lax.fori_loop(i * chunk, (i + 1) * chunk, place, 0)
 
-    @pl.when(core[0] == 0)
-    def _():
-        for copy in straight:
-            copy.wait()
-
-    @pl.when(core[0] != 0)
-    def _():
-        for copy in crossed:
-            copy.wait()
-
-    for at in range(0, rows, rows // 2):
-        part = slice(at, at + rows // 2)
+    for i, part in enumerate(steps):
+        on_operands(lambda copy: copy.wait(), i)
         pre = jnp.dot(x[part, :], up[...], preferred_element_type=jnp.float32)
         bent = bent_tanh(pre)
         unit = 0.5 * pre * (1.0 + bent)
@@ -137,9 +132,7 @@
         back = lax.dot_general(
             dy[part, :], down[...], (((1,), (1,)), ((), ())), preferred_element_type=jnp.float32
         )
-        grad[part, :] = (back * gelu_slope(pre, bent)).astype(jnp.bfloat16)
-    for at in range(0, width, 2 * half):
-        x_t[at : at + 2 * half, :] = jnp.transpose(x[:, at : at + 2 * half])
+        grad[:, part] = jnp.transpose(back * gelu_slope(pre, bent)).astype(jnp.bfloat16)
 
     def term(s, _):
         row, column = lax.div(down_index[s], per_row), lax.rem(down_index[s], per_row)
@@ -147,9 +140,9 @@
             hidden_t[span(column, half), :], dy[:, span(row, 2 * half)], preferred_element_type=jnp.float32
         ) * (s < down_count[0]).astype(jnp.float32)
         row, column = lax.div(up_index[s], per_row), lax.rem(up_index[s], per_row)
-        up_term = jnp.dot(
-            x_t[span(row, 2 * half), :], grad[:, span(column, half)], preferred_element_type=jnp.float32
-        ) * (s < up_count[0]).astype(jnp.float32)
+        up_term = jnp.transpose(jnp.dot(
+            grad[span(column, half), :], x[:, span(row, 2 * half)], preferred_element_type=jnp.float32
+        )) * (s < up_count[0]).astype(jnp.float32)
         held[:, s] = sent_rows(up_term, down_term, ring)
         return 0
 
@@ -196,9 +189,9 @@
             pltpu.VMEM((width, rows), jnp.bfloat16),
             pltpu.VMEM((width, units), jnp.bfloat16),
             pltpu.VMEM((units, width), jnp.bfloat16),
-            pltpu.VMEM((rows, units), jnp.bfloat16),
             pltpu.VMEM((units, rows), jnp.bfloat16),
-            pltpu.SemaphoreType.DMA((CHUNKS + 2,)),
+            pltpu.VMEM((units, rows), jnp.bfloat16),
+            pltpu.SemaphoreType.DMA((CHUNKS + 2 * STEPS,)),
             pltpu.SemaphoreType.DMA((CHUNKS,)),
         ],
         compiler_params=pltpu.CompilerParams(vmem_limit_bytes=VMEM_BYTES),
@@ -261,9 +254,16 @@
     summed = lax.psum_scatter(
         terms.reshape(ring * cap * 4 * part, half), RING, scatter_dimension=0, tiled=True
     ).reshape(cap, 4 * part, half)
-    value = partial_sum(down_index, down_count, hidden, slots, width).reshape(members, rows, width)
-    got = lax.all_to_all(value, (PAIR, PLANE, CORE), split_axis=0, concat_axis=0, tiled=True)
-    mixed = jnp.sum(got.astype(jnp.float32), axis=0).astype(jnp.bfloat16)
+    value = partial_sum(down_index, down_count, hidden, slots, width).reshape(shards, 2, rows, width)
+
+    def over_plane(value):
+        keep = lax.dynamic_index_in_dim(value, core, axis=1, keepdims=False)
+        send = lax.dynamic_index_in_dim(value, 1 - core, axis=1, keepdims=False)
+        added = (keep.astype(jnp.float32) + swapped(send, CORE).astype(jnp.float32)).astype(jnp.bfloat16)
+        got = lax.all_to_all(added, (PAIR, PLANE), split_axis=0, concat_axis=0, tiled=True)
+        return jnp.sum(got.astype(jnp.float32), axis=0).astype(jnp.bfloat16)
+
+    mixed = lax.cond(up_count[0] > 0, over_plane, lambda value: value[0, 0], value)
     low, high = summed[:, :part], summed[:, part : 2 * part]
     far = swapped(jnp.where(second, low, high), PAIR)
     near = jnp.where(second, high, low)

time: 199 us -> 195 us (0.980)
  blocking collectives: 126 us -> 100 us
  waiting for transfers between devices: 13.5 us -> 34.7 us
  local copies, waits for them, and re-layouts: 1.94 us -> 5.21 us
  starting transfers between devices: 8.85 us -> 10.9 us
    all_to_all x2 -> x1, blocking collectives: 126 us -> 63.9 us  [body(): lax.all_to_all(value, (PAIR, PLANE, CORE), split_axis=0, concat_axis=0, t...]
    all_to_all x0 -> x1, blocking collectives: none -> 36.5 us  [over_plane(): lax.all_to_all(added, (PAIR, PLANE), split_axis=0, concat_axis=0, tiled=T...]
    reduce_scatter x1, waiting for transfers between devices: 0.01 us -> 16.6 us  [body(): lax.psum_scatter(terms.reshape(ring * cap * 4 * part, half), RING, scatte...]
    ppermute x3 -> x4, waiting for transfers between devices: 9.76 us -> 14.4 us  [swapped(): return lax.ppermute(value, axis, [(0, 1), (1, 0)])]
    reduce_sum x1, other arithmetic: 3.92 us -> 0.39 us  [over_plane(): return jnp.sum(got.astype(jnp.float32), axis=0).astype(jnp.bfloat16)]
    squeeze x0 -> x1, local copies, waits for them, and re-layouts: none -> 3.26 us  [over_plane(): send = lax.dynamic_index_in_dim(value, 1 - core, axis=1, keepdims=False)]
    convert_element_type x0 -> x1, other arithmetic: none -> 2.55 us  [over_plane(): (keep.astype(jnp.float32) + swapped(send, CORE).astype(jnp.float32)).asty...]
    ppermute x3 -> x4, starting transfers between devices: 8.78 us -> 10.8 us  [swapped(): return lax.ppermute(value, axis, [(0, 1), (1, 0)])]
  transfers between devices with their start and end apart: 5 -> 6, of which waited for: 4 -> 6; matrix products, arithmetic and copies ran while one was open for 4% -> 5% of each run, Pallas kernels for 3% -> 3%
where the time goes in v4:
time: 195 us
  blocking collectives  100 us (51%)
  waiting for transfers between devices  34.7 us (18%)
  Pallas kernels  19.1 us (10%)
  between operations  15.4 us (8%)
  starting transfers between devices  10.9 us (6%)
  other arithmetic  8.8 us (5%)
  local copies, waits for them, and re-layouts  5.21 us (3%)
    all_to_all x1, blocking collectives, body(): lax.all_to_all(value, (PAIR, PLANE, CORE), split_axis=0, concat_axis=0, t...  63.9 us
    all_to_all x1, blocking collectives, over_plane(): lax.all_to_all(added, (PAIR, PLANE), split_axis=0, concat_axis=0, tiled=T...  36.5 us
    reduce_scatter x1, waiting for transfers between devices, body(): lax.psum_scatter(terms.reshape(ring * cap * 4 * part, half), RING, scatte...  16.6 us
    ppermute x4, waiting for transfers between devices, swapped(): return lax.ppermute(value, axis, [(0, 1), (1, 0)])  14.4 us
    pallas_call x1, Pallas kernels, all_terms(): pl.pallas_call(terms_kernel, out_shape=(pltpu.HBM(slots.shape, jnp.bfloat...  13.1 us
    ppermute x4, starting transfers between devices, swapped(): return lax.ppermute(value, axis, [(0, 1), (1, 0)])  10.8 us
    pallas_call x1, Pallas kernels, partial_sum(): pl.pallas_call(partial_kernel, out_shape=pltpu.HBM((rows, width), jnp.bfl...  5.94 us
  transfers between devices with their start and end apart: 6, of which 6 were waited for; matrix products, arithmetic and copies ran while one was open for 5% of the time, Pallas kernels for 3%

profile of v4, /device:TPU:6, one launch (start us, length us, event | category | flops | bytes accessed | tf_op | source)
XLA Modules:
  0.0 194.6 jit_solution(12645722029790350695)
XLA Ops:
  7.2 0.0 all-gather.2.cloned.1.call-start
  7.2 0.8 broadcast_select_fusion.5
  8.0 3.5 %collective-permute-start.2 = (bf16[20,8,128]{2,1,0:T(8,128)(2,1)S(1)}, bf16[20,8,128]{2,1,0:T(8,128)(2,1)S(1)}, u32[]{:S(2)}, u32[]{:S(2)}) collective-permute-start(bf16[20,8,128]{2,1,0:T(8,128)(2,1)S(1)} %get-tuple-element.34), channel_id=1, source_target_pairs={{0,256},{256,0},{1,257},{257,1},{2,258},{258,2},{3,259},{259,3},{4... | collective-permute-start | bytes 122888 | tf_op jit(solution)/shard_map/ppermute | solution.py:220
  11.5 0.8 fusion.3
  13.0 0.1 broadcast_in_dim.92
  13.1 0.1 broadcast_in_dim.93
  13.2 0.1 broadcast_in_dim.82
  13.3 0.1 broadcast_in_dim.83
  13.4 0.1 broadcast_in_dim.85
  13.5 0.1 broadcast_in_dim.86
  13.6 0.4 collective-permute-done.2
  13.9 1.0 fusion.1
  14.9 0.0 all-gather.2.cloned.1.call-update
  14.9 0.0 reduce-scatter.2.cloned.1.call-start
  15.0 1.0 pad_maximum_fusion
  16.0 0.0 copy-start.1
  16.0 0.0 copy-start.2
  16.0 64.5 %conditional.2 = (bf16[768,3072]{1,0:T(8,128)(2,1)}) conditional(s32[]{:T(128)} %bitcast.7, bf16[2,24,3072]{2,1,0:T(8,128)(2,1)S(1)} %pad_maximum_fusion, bf16[2,24,3072]{2,1,0:T(8,128)(2,1)S(1)} %pad_maximum_fusion), branch_computations={%region_0.1_spmd, %region_1.2_spmd} | conditional | bytes 14450696 | solution.py:244
  16.0 0.6 broadcast_in_dim.64
  16.6 63.9 %all_to_all.8 = bf16[32,24,3072]{2,1,0:T(8,128)(2,1)} all-to-all(bf16[32,24,3072]{2,1,0:T(8,128)(2,1)S(1)} %bitcast.34), channel_id=1, replica_groups=mesh['y_lo'=2,'z'=16,'yx'=8,'core'=2] {'y_lo','yx','core'}, dimensions={0} | all-to-all | bytes 9437184 | tf_op jit(solution)/shard_map/cond/branch_1_fun/all_to_all | solution.py:246
  80.5 2.3 %collective-permute-start.1 = (bf16[768,3072]{1,0:T(8,128)(2,1)}, bf16[768,3072]{1,0:T(8,128)(2,1)}, u32[]{:S(2)}, u32[]{:S(2)}) collective-permute-start(bf16[768,3072]{1,0:T(8,128)(2,1)} %get-tuple-element.37.mine), channel_id=1, source_target_pairs={{0,1},{1,0},{2,3},{3,2},{4,5},{5,4},{6,7},{7,6},{8,9},{9,8},{10,11... | collective-permute-start | bytes 14155784 | tf_op jit(solution)/shard_map/ppermute | solution.py:220
  83.5 7.2 %collective-permute-done.1.other = bf16[768,3072]{1,0:T(8,128)(2,1)} collective-permute-done((bf16[768,3072]{1,0:T(8,128)(2,1)}, bf16[768,3072]{1,0:T(8,128)(2,1)}, u32[]{:S(2)}, u32[]{:S(2)}) %collective-permute-start.1) | collective-permute-done | bytes 4718624 | tf_op jit(solution)/shard_map/ppermute | solution.py:220
  90.7 3.7 %all-gather.2.cloned.1.call-done = bf16[10240,128]{1,0:T(8,128)(2,1)} async-done(((bf16[640,128]{1,0:T(8,128)(2,1)}), bf16[10240,128]{1,0:T(8,128)(2,1)}) %all-gather.2.cloned.1.call-update) | async-done | bytes 2621456 | tf_op jit(solution)/shard_map/all_gather | solution.py:242
  94.3 0.0 copy-done.1
  94.3 0.0 copy-done.2
  94.3 0.0 copy-start
  94.3 13.1 %terms.1 = (bf16[16,20,32,128]{3,2,1,0:T(8,128)(2,1)}, bf16[768,384]{1,0:T(8,128)(2,1)S(1)}) custom-call(s32[20]{0:T(128)S(1)} %copy-done.2, s32[1]{0:T(128)S(6)} %copy.15.up_count, s32[20]{0:T(128)S(1)} %copy-done.1, s32[1]{0:T(128)S(6)} %copy.16.down_count, s32[1]{0:T(128)} %bitcast.8.core, bf16[768,3072]{1,0:T(8,128)(2,1)} %get-tuple-element.37.mine, ...), custom_call_target="tpu_custom_call" | custom-call | flops 5637144576 | bytes 5242880 | tf_op jit(solution)/shard_map/terms/pallas_call | solution.py:177
  107.5 0.0 reduce-scatter.2.cloned.1.call-update
  107.5 0.0 copy-done
  107.5 5.9 %partial.1 = bf16[768,3072]{1,0:T(8,128)(2,1)} custom-call(s32[20]{0:T(128)S(1)} %copy-done.1, s32[1]{0:T(128)S(6)} %copy.16.down_count, bf16[768,384]{1,0:T(8,128)(2,1)S(1)} %get-tuple-element.26.hidden, bf16[16,20,32,128]{3,2,1,0:T(8,128)(2,1)S(1)} %bitcast.31), custom_call_target="tpu_custom_call" | custom-call | flops 1811939328 | bytes 2621440 | tf_op jit(solution)/shard_map/partial/pallas_call | solution.py:205
  113.5 49.4 %conditional.3 = (bf16[24,3072]{1,0:T(8,128)(2,1)S(1)}) conditional(s32[]{:T(128)} %bitcast.7, bf16[16,2,24,3072]{3,2,1,0:T(8,128)(2,1)} %bitcast.32, (s32[]{:T(128)}, bf16[16,2,24,3072]{3,2,1,0:T(8,128)(2,1)}) %tuple.37), branch_computations={%region_2.3_spmd, %region_3.5_spmd} | conditional | flops 5824519 | bytes 28459146 | solution.py:266
  113.5 3.3 %dynamic-slice_bitcast_fusion = bf16[16,24,3072]{2,1,0:T(8,128)(2,1)} fusion(bf16[16,2,24,3072]{3,2,1,0:T(8,128)(2,1)} %get-tuple-element.19, s32[]{:T(128)S(6)} %select_n.38), kind=kLoop, calls=%fused_computation.3 | loop fusion | bytes 4718596 | tf_op jit(solution)/shard_map/cond/branch_1_fun/jit(dynamic_index_in_dim)/squeeze | solution.py:261
  116.7 1.9 collective-permute-start
  118.6 4.7 %collective-permute-done = bf16[16,24,3072]{2,1,0:T(8,128)(2,1)S(1)} collective-permute-done((bf16[16,24,3072]{2,1,0:T(8,128)(2,1)}, bf16[16,24,3072]{2,1,0:T(8,128)(2,1)S(1)}, u32[]{:S(2)}, u32[]{:S(2)}) %collective-permute-start) | collective-permute-done | bytes 2359328 | tf_op jit(solution)/shard_map/cond/branch_1_fun/ppermute | solution.py:220
  123.3 2.5 %fusion = bf16[16,24,3072]{2,1,0:T(8,128)(2,1)S(1)} fusion(bf16[16,24,3072]{2,1,0:T(8,128)(2,1)S(1)} %collective-permute-done, bf16[16,2,24,3072]{3,2,1,0:T(8,128)(2,1)} %get-tuple-element.19, s32[]{:T(128)S(6)} %select_n.37), kind=kLoop, calls=%fused_computation.2 | loop fusion | flops 4718592 | bytes 7077892 | tf_op jit(solution)/shard_map/cond/branch_1_fun/convert_element_type | solution.py:262
  125.9 36.5 %all_to_all.9 = bf16[16,24,3072]{2,1,0:T(8,128)(2,1)S(1)} all-to-all(bf16[16,24,3072]{2,1,0:T(8,128)(2,1)S(1)} %fusion), channel_id=1, replica_groups=mesh['y_lo'=2,'z'=16,'yx'=8,'core'=2] {'y_lo','yx'}, dimensions={0} | all-to-all | bytes 4718592 | tf_op jit(solution)/shard_map/cond/branch_1_fun/all_to_all | solution.py:263
  162.4 0.4 reduce_sum.11
  162.8 0.0 copy-start.3
  162.8 16.6 %reduce-scatter.2.cloned.1.call-done = bf16[640,128]{1,0:T(8,128)(2,1)} async-done(((bf16[10240,128]{1,0:T(8,128)(2,1)}), bf16[640,128]{1,0:T(8,128)(2,1)}) %reduce-scatter.2.cloned.1.call-update) | async-done | bytes 163856 | tf_op jit(solution)/shard_map/reduce_scatter | solution.py:254
  179.5 0.9 fusion.2
  180.3 3.1 %collective-permute-start.3 = (bf16[20,8,128]{2,1,0:T(8,128)(2,1)S(1)}, bf16[20,8,128]{2,1,0:T(8,128)(2,1)S(1)}, u32[]{:S(2)}, u32[]{:S(2)}) collective-permute-start(bf16[20,8,128]{2,1,0:T(8,128)(2,1)S(1)} %get-tuple-element.32), channel_id=1, source_target_pairs={{0,256},{256,0},{1,257},{257,1},{2,258},{258,2},{3,259},{259,3},{4... | collective-permute-start | bytes 122888 | tf_op jit(solution)/shard_map/ppermute | solution.py:220
  183.5 0.7 maximum_convert_fusion.1
  184.1 2.1 %collective-permute-done.3 = bf16[20,8,128]{2,1,0:T(8,128)(2,1)S(1)} collective-permute-done((bf16[20,8,128]{2,1,0:T(8,128)(2,1)S(1)}, bf16[20,8,128]{2,1,0:T(8,128)(2,1)S(1)}, u32[]{:S(2)}, u32[]{:S(2)}) %collective-permute-start.3) | collective-permute-done | bytes 40992 | tf_op jit(solution)/shard_map/ppermute | solution.py:220
  186.2 0.8 broadcast_select_fusion.1
  187.0 0.7 maximum_convert_fusion
  187.7 0.0 copy-done.3
  (3 shorter events, 0.0 us)
Async XLA Ops:
  7.2 87.2 %all-gather.2.cloned.1.call-start = ((), (), s32[]{:S(2)}) async-start(), calls=%async_computation.3 | async-start | bytes 2785280 | tf_op jit(solution)/shard_map/all_gather | solution.py:242
  8.0 5.9 %collective-permute-start.2 = (bf16[20,8,128]{2,1,0:T(8,128)(2,1)S(1)}, bf16[20,8,128]{2,1,0:T(8,128)(2,1)S(1)}, u32[]{:S(2)}, u32[]{:S(2)}) collective-permute-start(bf16[20,8,128]{2,1,0:T(8,128)(2,1)S(1)} %get-tuple-element.34), channel_id=1, source_target_pairs={{0,256},{256,0},{1,257},{257,1},{2,258},{258,2},{3,259},{259,3},{4... | collective-permute-start | bytes 122888 | tf_op jit(solution)/shard_map/ppermute | solution.py:220
  14.9 164.5 %reduce-scatter.2.cloned.1.call-start = ((), (), s32[]{:S(2)}) async-start(), calls=%async_computation.4 | async-start | bytes 2785280 | tf_op jit(solution)/shard_map/reduce_scatter | solution.py:254
  16.0 78.3 %copy-start.1 = (s32[20]{0:T(128)S(1)}, s32[20]{0:T(128)}, u32[]{:S(2)}) copy-start(s32[20]{0:T(128)} %down_index.3) | copy-start | bytes 244
  16.0 78.3 %copy-start.2 = (s32[20]{0:T(128)S(1)}, s32[20]{0:T(128)}, u32[]{:S(2)}) copy-start(s32[20]{0:T(128)} %up_index.1) | copy-start | bytes 244
  80.5 10.1 %collective-permute-start.1 = (bf16[768,3072]{1,0:T(8,128)(2,1)}, bf16[768,3072]{1,0:T(8,128)(2,1)}, u32[]{:S(2)}, u32[]{:S(2)}) collective-permute-start(bf16[768,3072]{1,0:T(8,128)(2,1)} %get-tuple-element.37.mine), channel_id=1, source_target_pairs={{0,1},{1,0},{2,3},{3,2},{4,5},{5,4},{6,7},{7,6},{8,9},{9,8},{10,11... | collective-permute-start | bytes 14155784 | tf_op jit(solution)/shard_map/ppermute | solution.py:220
  94.3 13.2 %copy-start = (bf16[10240,128]{1,0:T(8,128)(2,1)S(1)}, bf16[10240,128]{1,0:T(8,128)(2,1)}, u32[]{:S(2)}) copy-start(bf16[10240,128]{1,0:T(8,128)(2,1)} %all-gather.2.cloned.1.call-done) | copy-start | bytes 7864324
  116.7 6.6 %collective-permute-start = (bf16[16,24,3072]{2,1,0:T(8,128)(2,1)}, bf16[16,24,3072]{2,1,0:T(8,128)(2,1)S(1)}, u32[]{:S(2)}, u32[]{:S(2)}) collective-permute-start(bf16[16,24,3072]{2,1,0:T(8,128)(2,1)} %dynamic-slice_bitcast_fusion), channel_id=1, source_target_pairs={{0,1},{1,0},{2,3},{3,2},{4,5},{5,4},{6,7},{7,6},{8,9},{9,8},{10,11... | collective-permute-start | bytes 7077896 | tf_op jit(solution)/shard_map/cond/branch_1_fun/ppermute | solution.py:220
  162.8 24.9 %copy-start.3 = (bf16[24,3072]{1,0:T(8,128)(2,1)}, bf16[24,3072]{1,0:T(8,128)(2,1)S(1)}, u32[]{:S(2)}) copy-start(bf16[24,3072]{1,0:T(8,128)(2,1)S(1)} %get-tuple-element.38) | copy-start | bytes 442372
  180.3 5.9 %collective-permute-start.3 = (bf16[20,8,128]{2,1,0:T(8,128)(2,1)S(1)}, bf16[20,8,128]{2,1,0:T(8,128)(2,1)S(1)}, u32[]{:S(2)}, u32[]{:S(2)}) collective-permute-start(bf16[20,8,128]{2,1,0:T(8,128)(2,1)S(1)} %get-tuple-element.32), channel_id=1, source_target_pairs={{0,256},{256,0},{1,257},{257,1},{2,258},{258,2},{3,259},{259,3},{4... | collective-permute-start | bytes 122888 | tf_op jit(solution)/shard_map/ppermute | solution.py:220
Sparse Core Ops, SparseCore 0:
  15.1 79.2 all-gather.1
  107.6 71.7 reduce-scatter.1

commit v5 on v4

--- a/solution.py
+++ b/solution.py
@@ -230,9 +230,7 @@
     left, right = up_blocks[:, :, :half], up_blocks[:, :, half:]
     far = swapped(jnp.where(second, left, right), PAIR)
     near = jnp.where(second, right, left)
-    rows, width = tokens.shape
-    members = 2 * shards
-    both = jnp.broadcast_to(jnp.stack([tokens, cotangent])[None], (shards, 2, rows, width))
+    packed, far = lax.optimization_barrier((jnp.stack([tokens, cotangent]), far))
     number = jnp.arange(4)[None, :, None, None]
     quarters = jnp.where(
         number < 2,
@@ -241,12 +239,17 @@
     )
     slots = lax.all_gather(quarters.reshape(cap * 4 * part, half), RING, axis=0, tiled=True)
     slots = slots.reshape(ring, cap, 4 * part, half)
-    mine = lax.cond(
-        up_count[0] > 0,
-        lambda value: lax.all_to_all(value, (PAIR, PLANE, CORE), split_axis=0, concat_axis=0, tiled=True),
-        lambda value: value,
-        both.reshape(members, rows, width),
-    ).reshape(members * rows, width)
+    rows, width = tokens.shape
+    members = 2 * shards
+
+    def copies(value):
+        return jnp.broadcast_to(value[None], (shards,) + value.shape).reshape(members, rows, width)
+
+    def spread(value):
+        return lax.all_to_all(copies(value), (PAIR, PLANE, CORE), split_axis=0, concat_axis=0, tiled=True)
+
+    always = core < 2
+    mine = lax.cond(always, spread, copies, packed).reshape(members * rows, width)
     other = swapped(mine, CORE)
     terms, hidden = all_terms(
         up_index, up_count, down_index, down_count, core.reshape(1), mine, other, slots, FF // members
@@ -263,11 +266,10 @@
         got = lax.all_to_all(added, (PAIR, PLANE), split_axis=0, concat_axis=0, tiled=True)
         return jnp.sum(got.astype(jnp.float32), axis=0).astype(jnp.bfloat16)
 
-    mixed = lax.cond(up_count[0] > 0, over_plane, lambda value: value[0, 0], value)
+    mixed = lax.cond(always, over_plane, lambda value: value[0, 0], value)
     low, high = summed[:, :part], summed[:, part : 2 * part]
     far = swapped(jnp.where(second, low, high), PAIR)
-    near = jnp.where(second, high, low)
-    up_grad = jnp.concatenate([jnp.where(second, far, near), jnp.where(second, near, far)], axis=2)
+    up_grad = jnp.where(second, jnp.concatenate([far, high], axis=2), jnp.concatenate([low, far], axis=2))
     down_grad = jnp.concatenate([summed[:, 2 * part : 3 * part], summed[:, 3 * part :]], axis=2)
     return (mixed, up_grad.astype(jnp.float32), down_grad.astype(jnp.float32))
 

time: 195 us -> 194 us (level)
  transfers between devices with their start and end apart: 6 -> 6, of which waited for: 6 -> 5; matrix products, arithmetic and copies ran while one was open for 5% -> 5% of each run, Pallas kernels for 3% -> 3%
where the time goes in v5:
time: 194 us; the launch traced here: 193 us
  blocking collectives  99.9 us (51%)
  waiting for transfers between devices  34.5 us (18%)
  Pallas kernels  19.1 us (10%)
  between operations  15.5 us (8%)
  starting transfers between devices  11.2 us (6%)
  other arithmetic  8 us (4%)
  local copies, waits for them, and re-layouts  5.21 us (3%)
    all_to_all x1, blocking collectives, spread(): lax.all_to_all(copies(value), (PAIR, PLANE, CORE), split_axis=0, concat_a...  63.9 us
    all_to_all x1, blocking collectives, over_plane(): lax.all_to_all(added, (PAIR, PLANE), split_axis=0, concat_axis=0, tiled=T...  36.1 us
    reduce_scatter x1, waiting for transfers between devices, body(): lax.psum_scatter(terms.reshape(ring * cap * 4 * part, half), RING, scatte...  16.7 us
    pallas_call x1, Pallas kernels, all_terms(): pl.pallas_call(terms_kernel, out_shape=(pltpu.HBM(slots.shape, jnp.bfloat...  13.1 us
    ppermute x4, waiting for transfers between devices, swapped(): return lax.ppermute(value, axis, [(0, 1), (1, 0)])  13.1 us
    ppermute x4, starting transfers between devices, swapped(): return lax.ppermute(value, axis, [(0, 1), (1, 0)])  11.1 us
    pallas_call x1, Pallas kernels, partial_sum(): pl.pallas_call(partial_kernel, out_shape=pltpu.HBM((rows, width), jnp.bfl...  6.02 us
    all_gather x1, waiting for transfers between devices, body(): lax.all_gather(quarters.reshape(cap * 4 * part, half), RING, axis=0, tile...  4.7 us
  transfers between devices with their start and end apart: 6, of which 5 were waited for; matrix products, arithmetic and copies ran while one was open for 5% of the time, Pallas kernels for 3%

profile of v5, /device:TPU:6, one launch (start us, length us, event | category | flops | bytes accessed | tf_op | source)
XLA Modules:
  0.0 193.4 jit_solution(10418140227213612037)
XLA Ops:
  7.2 0.0 all-gather.2.cloned.1.call-start
  7.2 0.8 broadcast_select_fusion.1
  8.0 3.5 %collective-permute-start.1 = (bf16[20,8,128]{2,1,0:T(8,128)(2,1)S(1)}, bf16[20,8,128]{2,1,0:T(8,128)(2,1)S(1)}, u32[]{:S(2)}, u32[]{:S(2)}) collective-permute-start(bf16[20,8,128]{2,1,0:T(8,128)(2,1)S(1)} %get-tuple-element.33), channel_id=1, source_target_pairs={{0,256},{256,0},{1,257},{257,1},{2,258},{258,2},{3,259},{259,3},{4... | collective-permute-start | bytes 122888 | tf_op jit(solution)/shard_map/ppermute | solution.py:220
  11.5 0.8 fusion.4
  12.4 1.0 pad_maximum_fusion
  13.4 0.1 broadcast_in_dim.94
  13.5 0.1 broadcast_in_dim.95
  13.6 0.1 broadcast_in_dim.84
  13.6 0.1 broadcast_in_dim.85
  13.7 0.1 broadcast_in_dim.87
  13.8 0.1 broadcast_in_dim.88
  13.9 0.0 collective-permute-done.1
  13.9 1.0 fusion.1
  14.9 0.0 all-gather.2.cloned.1.call-update
  15.0 0.0 reduce-scatter.2.cloned.1.call-start
  15.0 0.0 copy-start.1
  15.0 0.0 copy-start.2
  15.0 64.5 %conditional.2 = (bf16[768,3072]{1,0:T(8,128)(2,1)}) conditional(s32[]{:T(128)} %convert_element_type.24, bf16[2,24,3072]{2,1,0:T(8,128)(2,1)S(1)} %pad_maximum_fusion, bf16[2,24,3072]{2,1,0:T(8,128)(2,1)S(1)} %pad_maximum_fusion), branch_computations={%region_0.1_spmd, %region_1.2_spmd} | conditional | bytes 14450696 | solution.py:252
  15.0 0.6 broadcast_in_dim.66
  15.6 63.9 %all_to_all.8 = bf16[32,24,3072]{2,1,0:T(8,128)(2,1)} all-to-all(bf16[32,24,3072]{2,1,0:T(8,128)(2,1)S(1)} %bitcast.33), channel_id=1, replica_groups=mesh['y_lo'=2,'z'=16,'yx'=8,'core'=2] {'y_lo','yx','core'}, dimensions={0} | all-to-all | bytes 9437184 | tf_op jit(solution)/shard_map/cond/branch_1_fun/all_to_all | solution.py:249
  79.5 2.3 %collective-permute-start.2 = (bf16[768,3072]{1,0:T(8,128)(2,1)}, bf16[768,3072]{1,0:T(8,128)(2,1)}, u32[]{:S(2)}, u32[]{:S(2)}) collective-permute-start(bf16[768,3072]{1,0:T(8,128)(2,1)} %get-tuple-element.36.mine), channel_id=1, source_target_pairs={{0,1},{1,0},{2,3},{3,2},{4,5},{5,4},{6,7},{7,6},{8,9},{9,8},{10,11... | collective-permute-start | bytes 14155784 | tf_op jit(solution)/shard_map/ppermute | solution.py:220
  83.1 6.6 %collective-permute-done.2.other = bf16[768,3072]{1,0:T(8,128)(2,1)} collective-permute-done((bf16[768,3072]{1,0:T(8,128)(2,1)}, bf16[768,3072]{1,0:T(8,128)(2,1)}, u32[]{:S(2)}, u32[]{:S(2)}) %collective-permute-start.2) | collective-permute-done | bytes 4718624 | tf_op jit(solution)/shard_map/ppermute | solution.py:220
  89.6 4.7 %all-gather.2.cloned.1.call-done = bf16[10240,128]{1,0:T(8,128)(2,1)} async-done(((bf16[640,128]{1,0:T(8,128)(2,1)}), bf16[10240,128]{1,0:T(8,128)(2,1)}) %all-gather.2.cloned.1.call-update) | async-done | bytes 2621456 | tf_op jit(solution)/shard_map/all_gather | solution.py:240
  94.3 0.0 copy-done.1
  94.3 0.0 copy-done.2
  94.3 0.0 copy-start
  94.3 13.1 %terms.1 = (bf16[16,20,32,128]{3,2,1,0:T(8,128)(2,1)}, bf16[768,384]{1,0:T(8,128)(2,1)S(1)}) custom-call(s32[20]{0:T(128)S(1)} %copy-done.2, s32[1]{0:T(128)S(6)} %copy.15.up_count, s32[20]{0:T(128)S(1)} %copy-done.1, s32[1]{0:T(128)S(6)} %copy.16.down_count, s32[1]{0:T(128)} %bitcast.7.core, bf16[768,3072]{1,0:T(8,128)(2,1)} %get-tuple-element.36.mine, ...), custom_call_target="tpu_custom_call" | custom-call | flops 5637144576 | bytes 5242880 | tf_op jit(solution)/shard_map/terms/pallas_call | solution.py:177
  107.5 0.0 reduce-scatter.2.cloned.1.call-update
  107.5 0.0 copy-done
  107.5 6.0 %partial.1 = bf16[768,3072]{1,0:T(8,128)(2,1)} custom-call(s32[20]{0:T(128)S(1)} %copy-done.1, s32[1]{0:T(128)S(6)} %copy.16.down_count, bf16[768,384]{1,0:T(8,128)(2,1)S(1)} %get-tuple-element.25.hidden, bf16[16,20,32,128]{3,2,1,0:T(8,128)(2,1)S(1)} %bitcast.30), custom_call_target="tpu_custom_call" | custom-call | flops 1811939328 | bytes 2621440 | tf_op jit(solution)/shard_map/partial/pallas_call | solution.py:205
  113.5 48.9 %conditional.3 = (bf16[24,3072]{1,0:T(8,128)(2,1)S(1)}) conditional(s32[]{:T(128)} %convert_element_type.24, bf16[16,2,24,3072]{3,2,1,0:T(8,128)(2,1)} %bitcast.31, (s32[]{:T(128)}, bf16[16,2,24,3072]{3,2,1,0:T(8,128)(2,1)}) %tuple.40), branch_computations={%region_2.3_spmd, %region_3.5_spmd} | conditional | flops 5824519 | bytes 28459146 | solution.py:269
  113.5 3.3 %dynamic-slice_bitcast_fusion = bf16[16,24,3072]{2,1,0:T(8,128)(2,1)} fusion(bf16[16,2,24,3072]{3,2,1,0:T(8,128)(2,1)} %get-tuple-element.14, s32[]{:T(128)S(6)} %select_n.35), kind=kLoop, calls=%fused_computation.3 | loop fusion | bytes 4718596 | tf_op jit(solution)/shard_map/cond/branch_1_fun/jit(dynamic_index_in_dim)/squeeze | solution.py:264
  116.8 1.9 collective-permute-start
  118.7 4.7 %collective-permute-done = bf16[16,24,3072]{2,1,0:T(8,128)(2,1)S(1)} collective-permute-done((bf16[16,24,3072]{2,1,0:T(8,128)(2,1)}, bf16[16,24,3072]{2,1,0:T(8,128)(2,1)S(1)}, u32[]{:S(2)}, u32[]{:S(2)}) %collective-permute-start) | collective-permute-done | bytes 2359328 | tf_op jit(solution)/shard_map/cond/branch_1_fun/ppermute | solution.py:220
  123.4 2.5 %fusion = bf16[16,24,3072]{2,1,0:T(8,128)(2,1)S(1)} fusion(bf16[16,24,3072]{2,1,0:T(8,128)(2,1)S(1)} %collective-permute-done, bf16[16,2,24,3072]{3,2,1,0:T(8,128)(2,1)} %get-tuple-element.14, s32[]{:T(128)S(6)} %select_n.34), kind=kLoop, calls=%fused_computation.2 | loop fusion | flops 4718592 | bytes 7077892 | tf_op jit(solution)/shard_map/cond/branch_1_fun/convert_element_type | solution.py:265
  126.0 36.1 %all_to_all.9 = bf16[16,24,3072]{2,1,0:T(8,128)(2,1)S(1)} all-to-all(bf16[16,24,3072]{2,1,0:T(8,128)(2,1)S(1)} %fusion), channel_id=1, replica_groups=mesh['y_lo'=2,'z'=16,'yx'=8,'core'=2] {'y_lo','yx'}, dimensions={0} | all-to-all | bytes 4718592 | tf_op jit(solution)/shard_map/cond/branch_1_fun/all_to_all | solution.py:266
  162.0 0.4 reduce_sum.11
  162.4 0.0 copy-start.3
  162.4 16.7 %reduce-scatter.2.cloned.1.call-done = bf16[640,128]{1,0:T(8,128)(2,1)} async-done(((bf16[10240,128]{1,0:T(8,128)(2,1)}), bf16[640,128]{1,0:T(8,128)(2,1)}) %reduce-scatter.2.cloned.1.call-update) | async-done | bytes 163856 | tf_op jit(solution)/shard_map/reduce_scatter | solution.py:257
  179.1 0.9 fusion.3
  180.0 3.4 %collective-permute-start.3 = (bf16[20,8,128]{2,1,0:T(8,128)(2,1)S(1)}, bf16[20,8,128]{2,1,0:T(8,128)(2,1)S(1)}, u32[]{:S(2)}, u32[]{:S(2)}) collective-permute-start(bf16[20,8,128]{2,1,0:T(8,128)(2,1)S(1)} %get-tuple-element.28), channel_id=1, source_target_pairs={{0,256},{256,0},{1,257},{257,1},{2,258},{258,2},{3,259},{259,3},{4... | collective-permute-start | bytes 122888 | tf_op jit(solution)/shard_map/ppermute | solution.py:220
  183.4 0.7 maximum_convert_fusion
  184.1 1.8 collective-permute-done.3
  185.9 0.7 fusion.2
  186.5 0.0 copy-done.3
  (3 shorter events, 0.0 us)
Async XLA Ops:
  7.2 87.2 %all-gather.2.cloned.1.call-start = ((), (), s32[]{:S(2)}) async-start(), calls=%async_computation.3 | async-start | bytes 2785280 | tf_op jit(solution)/shard_map/all_gather | solution.py:240
  8.0 5.9 %collective-permute-start.1 = (bf16[20,8,128]{2,1,0:T(8,128)(2,1)S(1)}, bf16[20,8,128]{2,1,0:T(8,128)(2,1)S(1)}, u32[]{:S(2)}, u32[]{:S(2)}) collective-permute-start(bf16[20,8,128]{2,1,0:T(8,128)(2,1)S(1)} %get-tuple-element.33), channel_id=1, source_target_pairs={{0,256},{256,0},{1,257},{257,1},{2,258},{258,2},{3,259},{259,3},{4... | collective-permute-start | bytes 122888 | tf_op jit(solution)/shard_map/ppermute | solution.py:220
  15.0 164.2 %reduce-scatter.2.cloned.1.call-start = ((), (), s32[]{:S(2)}) async-start(), calls=%async_computation.4 | async-start | bytes 2785280 | tf_op jit(solution)/shard_map/reduce_scatter | solution.py:257
  15.0 79.3 %copy-start.1 = (s32[20]{0:T(128)S(1)}, s32[20]{0:T(128)}, u32[]{:S(2)}) copy-start(s32[20]{0:T(128)} %down_index.3) | copy-start | bytes 244
  15.0 79.3 %copy-start.2 = (s32[20]{0:T(128)S(1)}, s32[20]{0:T(128)}, u32[]{:S(2)}) copy-start(s32[20]{0:T(128)} %up_index.1) | copy-start | bytes 244
  79.5 10.1 %collective-permute-start.2 = (bf16[768,3072]{1,0:T(8,128)(2,1)}, bf16[768,3072]{1,0:T(8,128)(2,1)}, u32[]{:S(2)}, u32[]{:S(2)}) collective-permute-start(bf16[768,3072]{1,0:T(8,128)(2,1)} %get-tuple-element.36.mine), channel_id=1, source_target_pairs={{0,1},{1,0},{2,3},{3,2},{4,5},{5,4},{6,7},{7,6},{8,9},{9,8},{10,11... | collective-permute-start | bytes 14155784 | tf_op jit(solution)/shard_map/ppermute | solution.py:220
  94.3 13.1 %copy-start = (bf16[10240,128]{1,0:T(8,128)(2,1)S(1)}, bf16[10240,128]{1,0:T(8,128)(2,1)}, u32[]{:S(2)}) copy-start(bf16[10240,128]{1,0:T(8,128)(2,1)} %all-gather.2.cloned.1.call-done) | copy-start | bytes 7864324
  116.8 6.6 %collective-permute-start = (bf16[16,24,3072]{2,1,0:T(8,128)(2,1)}, bf16[16,24,3072]{2,1,0:T(8,128)(2,1)S(1)}, u32[]{:S(2)}, u32[]{:S(2)}) collective-permute-start(bf16[16,24,3072]{2,1,0:T(8,128)(2,1)} %dynamic-slice_bitcast_fusion), channel_id=1, source_target_pairs={{0,1},{1,0},{2,3},{3,2},{4,5},{5,4},{6,7},{7,6},{8,9},{9,8},{10,11... | collective-permute-start | bytes 7077896 | tf_op jit(solution)/shard_map/cond/branch_1_fun/ppermute | solution.py:220
  162.4 24.1 %copy-start.3 = (bf16[24,3072]{1,0:T(8,128)(2,1)}, bf16[24,3072]{1,0:T(8,128)(2,1)S(1)}, u32[]{:S(2)}) copy-start(bf16[24,3072]{1,0:T(8,128)(2,1)S(1)} %get-tuple-element.37) | copy-start | bytes 442372
  180.0 5.9 %collective-permute-start.3 = (bf16[20,8,128]{2,1,0:T(8,128)(2,1)S(1)}, bf16[20,8,128]{2,1,0:T(8,128)(2,1)S(1)}, u32[]{:S(2)}, u32[]{:S(2)}) collective-permute-start(bf16[20,8,128]{2,1,0:T(8,128)(2,1)S(1)} %get-tuple-element.28), channel_id=1, source_target_pairs={{0,256},{256,0},{1,257},{257,1},{2,258},{258,2},{3,259},{259,3},{4... | collective-permute-start | bytes 122888 | tf_op jit(solution)/shard_map/ppermute | solution.py:220
Sparse Core Ops, SparseCore 0:
  15.1 79.2 all-gather.1
  107.6 71.4 reduce-scatter.1

commit v6 on v5

--- a/solution.py
+++ b/solution.py
@@ -227,10 +227,10 @@
     half = block // 2
     second = lax.axis_index(PAIR) == 1
     core = lax.axis_index(CORE)
-    left, right = up_blocks[:, :, :half], up_blocks[:, :, half:]
-    far = swapped(jnp.where(second, left, right), PAIR)
-    near = jnp.where(second, right, left)
+    far = swapped(up_blocks, PAIR)
     packed, far = lax.optimization_barrier((jnp.stack([tokens, cotangent]), far))
+    far = jnp.where(second, far[:, :, half:], far[:, :, :half])
+    near = jnp.where(second, up_blocks[:, :, half:], up_blocks[:, :, :half])
     number = jnp.arange(4)[None, :, None, None]
     quarters = jnp.where(
         number < 2,

time: 194 us -> 194 us (level)
  transfers between devices with their start and end apart: 6 -> 6, of which waited for: 5 -> 5; matrix products, arithmetic and copies ran while one was open for 5% -> 6% of each run, Pallas kernels for 3% -> 3%
where the time goes in v6:
time: 194 us; the launch traced here: 193 us
  blocking collectives  99.8 us (51%)
  waiting for transfers between devices  34.7 us (18%)
  Pallas kernels  19.1 us (10%)
  between operations  15.5 us (8%)
  starting transfers between devices  10.9 us (6%)
  other arithmetic  8.01 us (4%)
  local copies, waits for them, and re-layouts  5.21 us (3%)
    all_to_all x1, blocking collectives, spread(): lax.all_to_all(copies(value), (PAIR, PLANE, CORE), split_axis=0, concat_a...  63.7 us
    all_to_all x1, blocking collectives, over_plane(): lax.all_to_all(added, (PAIR, PLANE), split_axis=0, concat_axis=0, tiled=T...  36.1 us
    reduce_scatter x1, waiting for transfers between devices, body(): lax.psum_scatter(terms.reshape(ring * cap * 4 * part, half), RING, scatte...  16.6 us
    ppermute x4, waiting for transfers between devices, swapped(): return lax.ppermute(value, axis, [(0, 1), (1, 0)])  13.3 us
    pallas_call x1, Pallas kernels, all_terms(): pl.pallas_call(terms_kernel, out_shape=(pltpu.HBM(slots.shape, jnp.bfloat...  13.1 us
    ppermute x4, starting transfers between devices, swapped(): return lax.ppermute(value, axis, [(0, 1), (1, 0)])  10.8 us
    pallas_call x1, Pallas kernels, partial_sum(): pl.pallas_call(partial_kernel, out_shape=pltpu.HBM((rows, width), jnp.bfl...  6.02 us
    all_gather x1, waiting for transfers between devices, body(): lax.all_gather(quarters.reshape(cap * 4 * part, half), RING, axis=0, tile...  4.69 us
  transfers between devices with their start and end apart: 6, of which 5 were waited for; matrix products, arithmetic and copies ran while one was open for 6% of the time, Pallas kernels for 3%

profile of v6, /device:TPU:6, one launch (start us, length us, event | category | flops | bytes accessed | tf_op | source)
XLA Modules:
  0.0 193.2 jit_solution(7512704240609511447)
XLA Ops:
  7.2 0.0 all-gather.2.cloned.1.call-start
  7.2 3.5 %collective-permute-start.1 = (bf16[20,8,256]{2,1,0:T(8,128)(2,1)}, bf16[20,8,256]{2,1,0:T(8,128)(2,1)S(1)}, u32[]{:S(2)}, u32[]{:S(2)}) collective-permute-start(bf16[20,8,256]{2,1,0:T(8,128)(2,1)} %param.14), channel_id=1, source_target_pairs={{0,256},{256,0},{1,257},{257,1},{2,258},{258,2},{3,259},{259,3},{4... | collective-permute-start | bytes 245768 | tf_op jit(solution)/shard_map/ppermute | solution.py:220
  10.7 0.1 broadcast_in_dim.94
  10.8 0.1 broadcast_in_dim.95
  10.9 0.1 broadcast_in_dim.84
  11.0 0.1 broadcast_in_dim.85
  11.1 0.8 slice_select_fusion.1
  11.9 0.8 fusion.4
  12.7 1.0 pad_maximum_fusion
  13.7 0.1 broadcast_in_dim.87
  13.8 0.1 broadcast_in_dim.88
  13.9 0.0 collective-permute-done.1
  13.9 1.0 fusion.1
  14.9 0.0 all-gather.2.cloned.1.call-update
  15.0 0.0 reduce-scatter.2.cloned.1.call-start
  15.0 0.0 copy-start.1
  15.0 0.0 copy-start.2
  15.0 64.3 %conditional.2 = (bf16[768,3072]{1,0:T(8,128)(2,1)}) conditional(s32[]{:T(128)} %convert_element_type.24, bf16[2,24,3072]{2,1,0:T(8,128)(2,1)S(1)} %pad_maximum_fusion, bf16[2,24,3072]{2,1,0:T(8,128)(2,1)S(1)} %pad_maximum_fusion), branch_computations={%region_0.1_spmd, %region_1.2_spmd} | conditional | bytes 14450696 | solution.py:252
  15.0 0.6 broadcast_in_dim.66
  15.6 63.7 %all_to_all.8 = bf16[32,24,3072]{2,1,0:T(8,128)(2,1)} all-to-all(bf16[32,24,3072]{2,1,0:T(8,128)(2,1)S(1)} %bitcast.33), channel_id=1, replica_groups=mesh['y_lo'=2,'z'=16,'yx'=8,'core'=2] {'y_lo','yx','core'}, dimensions={0} | all-to-all | bytes 9437184 | tf_op jit(solution)/shard_map/cond/branch_1_fun/all_to_all | solution.py:249
  79.4 2.3 %collective-permute-start.2 = (bf16[768,3072]{1,0:T(8,128)(2,1)}, bf16[768,3072]{1,0:T(8,128)(2,1)}, u32[]{:S(2)}, u32[]{:S(2)}) collective-permute-start(bf16[768,3072]{1,0:T(8,128)(2,1)} %get-tuple-element.34.mine), channel_id=1, source_target_pairs={{0,1},{1,0},{2,3},{3,2},{4,5},{5,4},{6,7},{7,6},{8,9},{9,8},{10,11... | collective-permute-start | bytes 14155784 | tf_op jit(solution)/shard_map/ppermute | solution.py:220
  82.9 6.6 %collective-permute-done.2.other = bf16[768,3072]{1,0:T(8,128)(2,1)} collective-permute-done((bf16[768,3072]{1,0:T(8,128)(2,1)}, bf16[768,3072]{1,0:T(8,128)(2,1)}, u32[]{:S(2)}, u32[]{:S(2)}) %collective-permute-start.2) | collective-permute-done | bytes 4718624 | tf_op jit(solution)/shard_map/ppermute | solution.py:220
  89.5 4.7 %all-gather.2.cloned.1.call-done = bf16[10240,128]{1,0:T(8,128)(2,1)} async-done(((bf16[640,128]{1,0:T(8,128)(2,1)}), bf16[10240,128]{1,0:T(8,128)(2,1)}) %all-gather.2.cloned.1.call-update) | async-done | bytes 2621456 | tf_op jit(solution)/shard_map/all_gather | solution.py:240
  94.2 0.0 copy-done.1
  94.2 0.0 copy-done.2
  94.2 0.0 copy-start
  94.2 13.1 %terms.1 = (bf16[16,20,32,128]{3,2,1,0:T(8,128)(2,1)}, bf16[768,384]{1,0:T(8,128)(2,1)S(1)}) custom-call(s32[20]{0:T(128)S(1)} %copy-done.2, s32[1]{0:T(128)S(6)} %copy.15.up_count, s32[20]{0:T(128)S(1)} %copy-done.1, s32[1]{0:T(128)S(6)} %copy.16.down_count, s32[1]{0:T(128)} %bitcast.7.core, bf16[768,3072]{1,0:T(8,128)(2,1)} %get-tuple-element.34.mine, ...), custom_call_target="tpu_custom_call" | custom-call | flops 5637144576 | bytes 5242880 | tf_op jit(solution)/shard_map/terms/pallas_call | solution.py:177
  107.3 0.0 reduce-scatter.2.cloned.1.call-update
  107.3 0.0 copy-done
  107.3 6.0 %partial.1 = bf16[768,3072]{1,0:T(8,128)(2,1)} custom-call(s32[20]{0:T(128)S(1)} %copy-done.1, s32[1]{0:T(128)S(6)} %copy.16.down_count, bf16[768,384]{1,0:T(8,128)(2,1)S(1)} %get-tuple-element.25.hidden, bf16[16,20,32,128]{3,2,1,0:T(8,128)(2,1)S(1)} %bitcast.30), custom_call_target="tpu_custom_call" | custom-call | flops 1811939328 | bytes 2621440 | tf_op jit(solution)/shard_map/partial/pallas_call | solution.py:205
  113.3 48.9 %conditional.3 = (bf16[24,3072]{1,0:T(8,128)(2,1)S(1)}) conditional(s32[]{:T(128)} %convert_element_type.24, bf16[16,2,24,3072]{3,2,1,0:T(8,128)(2,1)} %bitcast.31, (s32[]{:T(128)}, bf16[16,2,24,3072]{3,2,1,0:T(8,128)(2,1)}) %tuple.39), branch_computations={%region_2.3_spmd, %region_3.5_spmd} | conditional | flops 5824519 | bytes 28459146 | solution.py:269
  113.3 3.3 %dynamic-slice_bitcast_fusion = bf16[16,24,3072]{2,1,0:T(8,128)(2,1)} fusion(bf16[16,2,24,3072]{3,2,1,0:T(8,128)(2,1)} %get-tuple-element.14, s32[]{:T(128)S(6)} %select_n.35), kind=kLoop, calls=%fused_computation.3 | loop fusion | bytes 4718596 | tf_op jit(solution)/shard_map/cond/branch_1_fun/jit(dynamic_index_in_dim)/squeeze | solution.py:264
  116.6 1.9 collective-permute-start
  118.5 4.7 %collective-permute-done = bf16[16,24,3072]{2,1,0:T(8,128)(2,1)S(1)} collective-permute-done((bf16[16,24,3072]{2,1,0:T(8,128)(2,1)}, bf16[16,24,3072]{2,1,0:T(8,128)(2,1)S(1)}, u32[]{:S(2)}, u32[]{:S(2)}) %collective-permute-start) | collective-permute-done | bytes 2359328 | tf_op jit(solution)/shard_map/cond/branch_1_fun/ppermute | solution.py:220
  123.2 2.5 %fusion = bf16[16,24,3072]{2,1,0:T(8,128)(2,1)S(1)} fusion(bf16[16,24,3072]{2,1,0:T(8,128)(2,1)S(1)} %collective-permute-done, bf16[16,2,24,3072]{3,2,1,0:T(8,128)(2,1)} %get-tuple-element.14, s32[]{:T(128)S(6)} %select_n.34), kind=kLoop, calls=%fused_computation.2 | loop fusion | flops 4718592 | bytes 7077892 | tf_op jit(solution)/shard_map/cond/branch_1_fun/convert_element_type | solution.py:265
  125.8 36.1 %all_to_all.9 = bf16[16,24,3072]{2,1,0:T(8,128)(2,1)S(1)} all-to-all(bf16[16,24,3072]{2,1,0:T(8,128)(2,1)S(1)} %fusion), channel_id=1, replica_groups=mesh['y_lo'=2,'z'=16,'yx'=8,'core'=2] {'y_lo','yx'}, dimensions={0} | all-to-all | bytes 4718592 | tf_op jit(solution)/shard_map/cond/branch_1_fun/all_to_all | solution.py:266
  161.9 0.4 reduce_sum.11
  162.3 0.0 copy-start.3
  162.3 16.6 %reduce-scatter.2.cloned.1.call-done = bf16[640,128]{1,0:T(8,128)(2,1)} async-done(((bf16[10240,128]{1,0:T(8,128)(2,1)}), bf16[640,128]{1,0:T(8,128)(2,1)}) %reduce-scatter.2.cloned.1.call-update) | async-done | bytes 163856 | tf_op jit(solution)/shard_map/reduce_scatter | solution.py:257
  178.9 0.9 fusion.3
  179.8 3.2 %collective-permute-start.3 = (bf16[20,8,128]{2,1,0:T(8,128)(2,1)S(1)}, bf16[20,8,128]{2,1,0:T(8,128)(2,1)S(1)}, u32[]{:S(2)}, u32[]{:S(2)}) collective-permute-start(bf16[20,8,128]{2,1,0:T(8,128)(2,1)S(1)} %get-tuple-element.28), channel_id=1, source_target_pairs={{0,256},{256,0},{1,257},{257,1},{2,258},{258,2},{3,259},{259,3},{4... | collective-permute-start | bytes 122888 | tf_op jit(solution)/shard_map/ppermute | solution.py:220
  183.0 0.7 maximum_convert_fusion
  183.6 2.1 %collective-permute-done.3 = bf16[20,8,128]{2,1,0:T(8,128)(2,1)S(1)} collective-permute-done((bf16[20,8,128]{2,1,0:T(8,128)(2,1)S(1)}, bf16[20,8,128]{2,1,0:T(8,128)(2,1)S(1)}, u32[]{:S(2)}, u32[]{:S(2)}) %collective-permute-start.3) | collective-permute-done | bytes 40992 | tf_op jit(solution)/shard_map/ppermute | solution.py:220
  185.7 0.7 fusion.2
  186.4 0.0 copy-done.3
  (4 shorter events, 0.0 us)
Async XLA Ops:
  7.2 87.0 %all-gather.2.cloned.1.call-start = ((), (), s32[]{:S(2)}) async-start(), calls=%async_computation.3 | async-start | bytes 2785280 | tf_op jit(solution)/shard_map/all_gather | solution.py:240
  7.2 6.7 %collective-permute-start.1 = (bf16[20,8,256]{2,1,0:T(8,128)(2,1)}, bf16[20,8,256]{2,1,0:T(8,128)(2,1)S(1)}, u32[]{:S(2)}, u32[]{:S(2)}) collective-permute-start(bf16[20,8,256]{2,1,0:T(8,128)(2,1)} %param.14), channel_id=1, source_target_pairs={{0,256},{256,0},{1,257},{257,1},{2,258},{258,2},{3,259},{259,3},{4... | collective-permute-start | bytes 245768 | tf_op jit(solution)/shard_map/ppermute | solution.py:220
  15.0 164.0 %reduce-scatter.2.cloned.1.call-start = ((), (), s32[]{:S(2)}) async-start(), calls=%async_computation.4 | async-start | bytes 2785280 | tf_op jit(solution)/shard_map/reduce_scatter | solution.py:257
  15.0 79.2 %copy-start.1 = (s32[20]{0:T(128)S(1)}, s32[20]{0:T(128)}, u32[]{:S(2)}) copy-start(s32[20]{0:T(128)} %down_index.3) | copy-start | bytes 244
  15.0 79.2 %copy-start.2 = (s32[20]{0:T(128)S(1)}, s32[20]{0:T(128)}, u32[]{:S(2)}) copy-start(s32[20]{0:T(128)} %up_index.1) | copy-start | bytes 244
  79.4 10.1 %collective-permute-start.2 = (bf16[768,3072]{1,0:T(8,128)(2,1)}, bf16[768,3072]{1,0:T(8,128)(2,1)}, u32[]{:S(2)}, u32[]{:S(2)}) collective-permute-start(bf16[768,3072]{1,0:T(8,128)(2,1)} %get-tuple-element.34.mine), channel_id=1, source_target_pairs={{0,1},{1,0},{2,3},{3,2},{4,5},{5,4},{6,7},{7,6},{8,9},{9,8},{10,11... | collective-permute-start | bytes 14155784 | tf_op jit(solution)/shard_map/ppermute | solution.py:220
  94.2 13.1 %copy-start = (bf16[10240,128]{1,0:T(8,128)(2,1)S(1)}, bf16[10240,128]{1,0:T(8,128)(2,1)}, u32[]{:S(2)}) copy-start(bf16[10240,128]{1,0:T(8,128)(2,1)} %all-gather.2.cloned.1.call-done) | copy-start | bytes 7864324
  116.6 6.6 %collective-permute-start = (bf16[16,24,3072]{2,1,0:T(8,128)(2,1)}, bf16[16,24,3072]{2,1,0:T(8,128)(2,1)S(1)}, u32[]{:S(2)}, u32[]{:S(2)}) collective-permute-start(bf16[16,24,3072]{2,1,0:T(8,128)(2,1)} %dynamic-slice_bitcast_fusion), channel_id=1, source_target_pairs={{0,1},{1,0},{2,3},{3,2},{4,5},{5,4},{6,7},{7,6},{8,9},{9,8},{10,11... | collective-permute-start | bytes 7077896 | tf_op jit(solution)/shard_map/cond/branch_1_fun/ppermute | solution.py:220
  162.3 24.1 %copy-start.3 = (bf16[24,3072]{1,0:T(8,128)(2,1)}, bf16[24,3072]{1,0:T(8,128)(2,1)S(1)}, u32[]{:S(2)}) copy-start(bf16[24,3072]{1,0:T(8,128)(2,1)S(1)} %get-tuple-element.35) | copy-start | bytes 442372
  179.8 5.9 %collective-permute-start.3 = (bf16[20,8,128]{2,1,0:T(8,128)(2,1)S(1)}, bf16[20,8,128]{2,1,0:T(8,128)(2,1)S(1)}, u32[]{:S(2)}, u32[]{:S(2)}) collective-permute-start(bf16[20,8,128]{2,1,0:T(8,128)(2,1)S(1)} %get-tuple-element.28), channel_id=1, source_target_pairs={{0,256},{256,0},{1,257},{257,1},{2,258},{258,2},{3,259},{259,3},{4... | collective-permute-start | bytes 122888 | tf_op jit(solution)/shard_map/ppermute | solution.py:220
Sparse Core Ops, SparseCore 0:
  15.1 79.0 all-gather.1
  107.4 71.4 reduce-scatter.1

commit v7 on v5

--- a/solution.py
+++ b/solution.py
@@ -230,13 +230,14 @@
     left, right = up_blocks[:, :, :half], up_blocks[:, :, half:]
     far = swapped(jnp.where(second, left, right), PAIR)
     near = jnp.where(second, right, left)
-    packed, far = lax.optimization_barrier((jnp.stack([tokens, cotangent]), far))
     number = jnp.arange(4)[None, :, None, None]
-    quarters = jnp.where(
+    laid = jnp.where(
         number < 2,
-        jnp.where((number == 1) == second, near[:, None], far[:, None]),
+        near[:, None],
         jnp.where(number == 2, down_blocks[:, None, :, :half], down_blocks[:, None, :, half:]),
     )
+    packed, laid, far = lax.optimization_barrier((jnp.stack([tokens, cotangent]), laid, far))
+    quarters = jnp.where((number < 2) & ((number == 1) != second), far[:, None], laid)
     slots = lax.all_gather(quarters.reshape(cap * 4 * part, half), RING, axis=0, tiled=True)
     slots = slots.reshape(ring, cap, 4 * part, half)
     rows, width = tokens.shape

time: 194 us -> 194 us (level)
  transfers between devices with their start and end apart: 6 -> 6, of which waited for: 5 -> 6; matrix products, arithmetic and copies ran while one was open for 5% -> 4% of each run, Pallas kernels for 3% -> 3%
where the time goes in v7:
time: 194 us; the launch traced here: 193 us
  blocking collectives  100 us (52%)
  waiting for transfers between devices  35.6 us (18%)
  Pallas kernels  18.9 us (10%)
  between operations  15.4 us (8%)
  starting transfers between devices  11 us (6%)
  other arithmetic  7.89 us (4%)
  local copies, waits for them, and re-layouts  3.86 us (2%)
    all_to_all x1, blocking collectives, spread(): lax.all_to_all(copies(value), (PAIR, PLANE, CORE), split_axis=0, concat_a...  63.9 us
    all_to_all x1, blocking collectives, over_plane(): lax.all_to_all(added, (PAIR, PLANE), split_axis=0, concat_axis=0, tiled=T...  36.4 us
    reduce_scatter x1, waiting for transfers between devices, body(): lax.psum_scatter(terms.reshape(ring * cap * 4 * part, half), RING, scatte...  16.4 us
    ppermute x4, waiting for transfers between devices, swapped(): return lax.ppermute(value, axis, [(0, 1), (1, 0)])  14.4 us
    pallas_call x1, Pallas kernels, all_terms(): pl.pallas_call(terms_kernel, out_shape=(pltpu.HBM(slots.shape, jnp.bfloat...  13.1 us
    ppermute x4, starting transfers between devices, swapped(): return lax.ppermute(value, axis, [(0, 1), (1, 0)])  11 us
    pallas_call x1, Pallas kernels, partial_sum(): pl.pallas_call(partial_kernel, out_shape=pltpu.HBM((rows, width), jnp.bfl...  5.87 us
    all_gather x1, waiting for transfers between devices, body(): lax.all_gather(quarters.reshape(cap * 4 * part, half), RING, axis=0, tile...  4.7 us
  transfers between devices with their start and end apart: 6, of which 6 were waited for; matrix products, arithmetic and copies ran while one was open for 4% of the time, Pallas kernels for 3%

profile of v7, /device:TPU:6, one launch (start us, length us, event | category | flops | bytes accessed | tf_op | source)
XLA Modules:
  0.0 193.1 jit_solution(1443285213676898330)
XLA Ops:
  7.2 0.0 all-gather.2.cloned.1.call-start
  7.2 0.9 broadcast_select_fusion.2
  8.1 3.5 %collective-permute-start.1 = (bf16[20,8,128]{2,1,0:T(8,128)(2,1)S(1)}, bf16[20,8,128]{2,1,0:T(8,128)(2,1)S(1)}, u32[]{:S(2)}, u32[]{:S(2)}) collective-permute-start(bf16[20,8,128]{2,1,0:T(8,128)(2,1)S(1)} %get-tuple-element.34), channel_id=1, source_target_pairs={{0,256},{256,0},{1,257},{257,1},{2,258},{258,2},{3,259},{259,3},{4... | collective-permute-start | bytes 122888 | tf_op jit(solution)/shard_map/ppermute | solution.py:220
  11.6 1.0 pad_maximum_fusion
  12.6 0.1 select_select_fusion
  12.7 1.3 collective-permute-done.1
  14.0 0.8 broadcast_select_fusion
  14.7 0.0 all-gather.2.cloned.1.call-update
  14.7 0.0 reduce-scatter.2.cloned.1.call-start
  14.8 0.0 copy-start.1
  14.8 0.0 copy-start.2
  14.8 64.5 %conditional.2 = (bf16[768,3072]{1,0:T(8,128)(2,1)}) conditional(s32[]{:T(128)} %convert_element_type.24, bf16[2,24,3072]{2,1,0:T(8,128)(2,1)S(1)} %pad_maximum_fusion, bf16[2,24,3072]{2,1,0:T(8,128)(2,1)S(1)} %pad_maximum_fusion), branch_computations={%region_0.1_spmd, %region_1.2_spmd} | conditional | bytes 14450696 | solution.py:253
  14.8 0.6 broadcast_in_dim.59
  15.4 63.9 %all_to_all.8 = bf16[32,24,3072]{2,1,0:T(8,128)(2,1)} all-to-all(bf16[32,24,3072]{2,1,0:T(8,128)(2,1)S(1)} %bitcast.22), channel_id=1, replica_groups=mesh['y_lo'=2,'z'=16,'yx'=8,'core'=2] {'y_lo','yx','core'}, dimensions={0} | all-to-all | bytes 9437184 | tf_op jit(solution)/shard_map/cond/branch_1_fun/all_to_all | solution.py:250
  79.3 2.3 %collective-permute-start.2 = (bf16[768,3072]{1,0:T(8,128)(2,1)}, bf16[768,3072]{1,0:T(8,128)(2,1)}, u32[]{:S(2)}, u32[]{:S(2)}) collective-permute-start(bf16[768,3072]{1,0:T(8,128)(2,1)} %get-tuple-element.42.mine), channel_id=1, source_target_pairs={{0,1},{1,0},{2,3},{3,2},{4,5},{5,4},{6,7},{7,6},{8,9},{9,8},{10,11... | collective-permute-start | bytes 14155784 | tf_op jit(solution)/shard_map/ppermute | solution.py:220
  82.9 6.6 %collective-permute-done.2.other = bf16[768,3072]{1,0:T(8,128)(2,1)} collective-permute-done((bf16[768,3072]{1,0:T(8,128)(2,1)}, bf16[768,3072]{1,0:T(8,128)(2,1)}, u32[]{:S(2)}, u32[]{:S(2)}) %collective-permute-start.2) | collective-permute-done | bytes 4718624 | tf_op jit(solution)/shard_map/ppermute | solution.py:220
  89.4 4.7 %all-gather.2.cloned.1.call-done = bf16[10240,128]{1,0:T(8,128)(2,1)} async-done(((bf16[640,128]{1,0:T(8,128)(2,1)}), bf16[10240,128]{1,0:T(8,128)(2,1)}) %all-gather.2.cloned.1.call-update) | async-done | bytes 2621456 | tf_op jit(solution)/shard_map/all_gather | solution.py:241
  94.1 0.0 copy-done.1
  94.1 0.0 copy-done.2
  94.1 0.0 copy-start
  94.1 13.1 %terms.1 = (bf16[16,20,32,128]{3,2,1,0:T(8,128)(2,1)}, bf16[768,384]{1,0:T(8,128)(2,1)S(1)}) custom-call(s32[20]{0:T(128)S(1)} %copy-done.2, s32[1]{0:T(128)S(6)} %copy.15.up_count, s32[20]{0:T(128)S(1)} %copy-done.1, s32[1]{0:T(128)S(6)} %copy.16.down_count, s32[1]{0:T(128)} %bitcast.7.core, bf16[768,3072]{1,0:T(8,128)(2,1)} %get-tuple-element.42.mine, ...), custom_call_target="tpu_custom_call" | custom-call | flops 5637144576 | bytes 5242880 | tf_op jit(solution)/shard_map/terms/pallas_call | solution.py:177
  107.2 0.0 reduce-scatter.2.cloned.1.call-update
  107.3 0.0 copy-done
  107.3 5.9 %partial.1 = bf16[768,3072]{1,0:T(8,128)(2,1)} custom-call(s32[20]{0:T(128)S(1)} %copy-done.1, s32[1]{0:T(128)S(6)} %copy.16.down_count, bf16[768,384]{1,0:T(8,128)(2,1)S(1)} %get-tuple-element.27.hidden, bf16[16,20,32,128]{3,2,1,0:T(8,128)(2,1)S(1)} %bitcast.19), custom_call_target="tpu_custom_call" | custom-call | flops 1811939328 | bytes 2621440 | tf_op jit(solution)/shard_map/partial/pallas_call | solution.py:205
  113.1 49.2 %conditional.3 = (bf16[24,3072]{1,0:T(8,128)(2,1)S(1)}) conditional(s32[]{:T(128)} %convert_element_type.24, bf16[16,2,24,3072]{3,2,1,0:T(8,128)(2,1)} %bitcast.20, (s32[]{:T(128)}, bf16[16,2,24,3072]{3,2,1,0:T(8,128)(2,1)}) %tuple.43), branch_computations={%region_2.3_spmd, %region_3.5_spmd} | conditional | flops 5824519 | bytes 28459146 | solution.py:270
  113.1 3.3 %dynamic-slice_bitcast_fusion = bf16[16,24,3072]{2,1,0:T(8,128)(2,1)} fusion(bf16[16,2,24,3072]{3,2,1,0:T(8,128)(2,1)} %get-tuple-element.14, s32[]{:T(128)S(6)} %select_n.32), kind=kLoop, calls=%fused_computation.3 | loop fusion | bytes 4718596 | tf_op jit(solution)/shard_map/cond/branch_1_fun/jit(dynamic_index_in_dim)/squeeze | solution.py:265
  116.4 1.9 collective-permute-start
  118.3 4.7 %collective-permute-done = bf16[16,24,3072]{2,1,0:T(8,128)(2,1)S(1)} collective-permute-done((bf16[16,24,3072]{2,1,0:T(8,128)(2,1)}, bf16[16,24,3072]{2,1,0:T(8,128)(2,1)S(1)}, u32[]{:S(2)}, u32[]{:S(2)}) %collective-permute-start) | collective-permute-done | bytes 2359328 | tf_op jit(solution)/shard_map/cond/branch_1_fun/ppermute | solution.py:220
  123.0 2.5 %fusion = bf16[16,24,3072]{2,1,0:T(8,128)(2,1)S(1)} fusion(bf16[16,24,3072]{2,1,0:T(8,128)(2,1)S(1)} %collective-permute-done, bf16[16,2,24,3072]{3,2,1,0:T(8,128)(2,1)} %get-tuple-element.14, s32[]{:T(128)S(6)} %select_n.31), kind=kLoop, calls=%fused_computation.2 | loop fusion | flops 4718592 | bytes 7077892 | tf_op jit(solution)/shard_map/cond/branch_1_fun/convert_element_type | solution.py:266
  125.6 36.4 %all_to_all.9 = bf16[16,24,3072]{2,1,0:T(8,128)(2,1)S(1)} all-to-all(bf16[16,24,3072]{2,1,0:T(8,128)(2,1)S(1)} %fusion), channel_id=1, replica_groups=mesh['y_lo'=2,'z'=16,'yx'=8,'core'=2] {'y_lo','yx'}, dimensions={0} | all-to-all | bytes 4718592 | tf_op jit(solution)/shard_map/cond/branch_1_fun/all_to_all | solution.py:267
  161.9 0.4 reduce_sum.11
  162.3 0.0 copy-start.3
  162.4 16.4 %reduce-scatter.2.cloned.1.call-done = bf16[640,128]{1,0:T(8,128)(2,1)} async-done(((bf16[10240,128]{1,0:T(8,128)(2,1)}), bf16[640,128]{1,0:T(8,128)(2,1)}) %reduce-scatter.2.cloned.1.call-update) | async-done | bytes 163856 | tf_op jit(solution)/shard_map/reduce_scatter | solution.py:258
  178.8 0.9 fusion.2
  179.7 3.3 %collective-permute-start.3 = (bf16[20,8,128]{2,1,0:T(8,128)(2,1)S(1)}, bf16[20,8,128]{2,1,0:T(8,128)(2,1)S(1)}, u32[]{:S(2)}, u32[]{:S(2)}) collective-permute-start(bf16[20,8,128]{2,1,0:T(8,128)(2,1)S(1)} %get-tuple-element.30), channel_id=1, source_target_pairs={{0,256},{256,0},{1,257},{257,1},{2,258},{258,2},{3,259},{259,3},{4... | collective-permute-start | bytes 122888 | tf_op jit(solution)/shard_map/ppermute | solution.py:220
  183.0 0.7 maximum_convert_fusion
  183.6 1.9 collective-permute-done.3
  185.6 0.7 fusion.1
  186.2 0.0 copy-done.3
  (2 shorter events, 0.0 us)
Async XLA Ops:
  7.2 87.0 %all-gather.2.cloned.1.call-start = ((), (), s32[]{:S(2)}) async-start(), calls=%async_computation.3 | async-start | bytes 2785280 | tf_op jit(solution)/shard_map/all_gather | solution.py:241
  8.1 5.9 %collective-permute-start.1 = (bf16[20,8,128]{2,1,0:T(8,128)(2,1)S(1)}, bf16[20,8,128]{2,1,0:T(8,128)(2,1)S(1)}, u32[]{:S(2)}, u32[]{:S(2)}) collective-permute-start(bf16[20,8,128]{2,1,0:T(8,128)(2,1)S(1)} %get-tuple-element.34), channel_id=1, source_target_pairs={{0,256},{256,0},{1,257},{257,1},{2,258},{258,2},{3,259},{259,3},{4... | collective-permute-start | bytes 122888 | tf_op jit(solution)/shard_map/ppermute | solution.py:220
  14.7 164.0 %reduce-scatter.2.cloned.1.call-start = ((), (), s32[]{:S(2)}) async-start(), calls=%async_computation.4 | async-start | bytes 2785280 | tf_op jit(solution)/shard_map/reduce_scatter | solution.py:258
  14.8 79.3 %copy-start.1 = (s32[20]{0:T(128)S(1)}, s32[20]{0:T(128)}, u32[]{:S(2)}) copy-start(s32[20]{0:T(128)} %down_index.3) | copy-start | bytes 244
  14.8 79.3 %copy-start.2 = (s32[20]{0:T(128)S(1)}, s32[20]{0:T(128)}, u32[]{:S(2)}) copy-start(s32[20]{0:T(128)} %up_index.1) | copy-start | bytes 244
  79.3 10.1 %collective-permute-start.2 = (bf16[768,3072]{1,0:T(8,128)(2,1)}, bf16[768,3072]{1,0:T(8,128)(2,1)}, u32[]{:S(2)}, u32[]{:S(2)}) collective-permute-start(bf16[768,3072]{1,0:T(8,128)(2,1)} %get-tuple-element.42.mine), channel_id=1, source_target_pairs={{0,1},{1,0},{2,3},{3,2},{4,5},{5,4},{6,7},{7,6},{8,9},{9,8},{10,11... | collective-permute-start | bytes 14155784 | tf_op jit(solution)/shard_map/ppermute | solution.py:220
  94.1 13.1 %copy-start = (bf16[10240,128]{1,0:T(8,128)(2,1)S(1)}, bf16[10240,128]{1,0:T(8,128)(2,1)}, u32[]{:S(2)}) copy-start(bf16[10240,128]{1,0:T(8,128)(2,1)} %all-gather.2.cloned.1.call-done) | copy-start | bytes 7864324
  116.4 6.6 %collective-permute-start = (bf16[16,24,3072]{2,1,0:T(8,128)(2,1)}, bf16[16,24,3072]{2,1,0:T(8,128)(2,1)S(1)}, u32[]{:S(2)}, u32[]{:S(2)}) collective-permute-start(bf16[16,24,3072]{2,1,0:T(8,128)(2,1)} %dynamic-slice_bitcast_fusion), channel_id=1, source_target_pairs={{0,1},{1,0},{2,3},{3,2},{4,5},{5,4},{6,7},{7,6},{8,9},{9,8},{10,11... | collective-permute-start | bytes 7077896 | tf_op jit(solution)/shard_map/cond/branch_1_fun/ppermute | solution.py:220
  162.3 23.9 %copy-start.3 = (bf16[24,3072]{1,0:T(8,128)(2,1)}, bf16[24,3072]{1,0:T(8,128)(2,1)S(1)}, u32[]{:S(2)}) copy-start(bf16[24,3072]{1,0:T(8,128)(2,1)S(1)} %get-tuple-element.43) | copy-start | bytes 442372
  179.7 5.9 %collective-permute-start.3 = (bf16[20,8,128]{2,1,0:T(8,128)(2,1)S(1)}, bf16[20,8,128]{2,1,0:T(8,128)(2,1)S(1)}, u32[]{:S(2)}, u32[]{:S(2)}) collective-permute-start(bf16[20,8,128]{2,1,0:T(8,128)(2,1)S(1)} %get-tuple-element.30), channel_id=1, source_target_pairs={{0,256},{256,0},{1,257},{257,1},{2,258},{258,2},{3,259},{259,3},{4... | collective-permute-start | bytes 122888 | tf_op jit(solution)/shard_map/ppermute | solution.py:220
Sparse Core Ops, SparseCore 0:
  14.9 79.2 all-gather.1
  107.4 71.3 reduce-scatter.1
